TPU v7x, 512 devices: a whole 4x8x8 slice. The times are simulated.
512 devices in a mesh: blk: 32 (over z, y_lo, core), head: 16 (over y_hi, x).
Axes of the slice: x: 4, y: 8 (y_hi: 4, y_lo: 2; y = y_hi * 2 + y_lo), z: 8, core: 2. Of those that a mesh axis runs over, the one named last changes fastest.
Arguments:
- queries: bfloat16 [4096, 4096], P('blk', 'head'), may hold values from -4 to 4
- keys: bfloat16 [4096, 4096], P('blk', 'head'), may hold values from -4 to 4
- values: bfloat16 [4096, 4096], P('blk', 'head'), may hold values from -6 to 6
- saved_out: bfloat16 [4096, 4096], P('blk', 'head'), may hold values from -6 to 6
- d_layer: bfloat16 [4096, 4096], P('blk', 'head'), may hold values from -6 to 6
- out_weight: bfloat16 [4096, 4096], P('head'), may hold values from -0.09375 to 0.09375
- prefix: int32 [1], replicated, may hold values from 512 to 3071
- block_order: int32 [64], replicated, may hold values from 0 to 63, each once
Outputs:
- grad_queries: bfloat16 [4096, 4096], P('blk', 'head')
- grad_keys: bfloat16 [4096, 4096], P('blk', 'head')
- grad_values: bfloat16 [4096, 4096], P('blk', 'head')
Inputs may be any that keep to these rules, and one draw needn't show every extreme that they name: `block_order`: a permutation of the 64 sequence blocks.
All inputs are finite; a program needn't handle non-finite values.
Results may differ from a plain program's by a relative error of at most 0.02.
Values may be sent and summed in bfloat16 or wider, within the bound.
A program may use at most 64 MiB of HBM per device.

v0:
```python
import jax
import jax.numpy as jnp
from jax import lax
from jax.sharding import PartitionSpec as P

HD = 256


score_floor = -1e30


def shifted(value, axis, steps):
    count = lax.axis_size(axis)
    pairs = [(source, (source + steps) % count) for source in range(count)]
    return lax.ppermute(value, axis, pairs)


def row_positions(block_order, first_row, row_count, block_rows):
    rows = first_row + jnp.arange(row_count, dtype=jnp.int32)
    owners = rows // block_rows
    blocks = jnp.arange(block_order.shape[0], dtype=jnp.int32)
    picked = jnp.sum(jnp.where(owners[:, None] == blocks[None, :], block_order[None, :], 0), axis=1)
    return picked * block_rows + rows % block_rows


def visible_pairs(query_pos, key_pos, prefix_len):
    return (key_pos[None, :] <= query_pos[:, None]) | (key_pos[None, :] < prefix_len)


def pair_gradients(
    query_rows,
    grad_rows,
    log_total,
    delta_rows,
    key_rows,
    value_rows,
    visible,
    head_count,
    score_scale,
):
    query_count = query_rows.shape[0]
    key_count = key_rows.shape[0]
    query_heads = query_rows.reshape(query_count, head_count, HD)
    grad_heads = grad_rows.reshape(query_count, head_count, HD)
    key_heads = key_rows.reshape(key_count, head_count, HD)
    value_heads = value_rows.reshape(key_count, head_count, HD)
    scores = (
        jnp.einsum("thd,shd->hts", query_heads, key_heads, preferred_element_type=jnp.float32)
        * score_scale
    )
    scores = jnp.where(visible[None], scores, score_floor)
    probs = jnp.where(visible[None], jnp.exp(scores - log_total[:, :, None]), 0.0)
    grad_value = jnp.einsum(
        "hts,thd->shd", probs.astype(jnp.bfloat16), grad_heads, preferred_element_type=jnp.float32
    )
    grad_probs = jnp.einsum(
        "thd,shd->hts", grad_heads, value_heads, preferred_element_type=jnp.float32
    )
    grad_scores = (probs * (grad_probs - delta_rows[:, :, None]) * score_scale).astype(jnp.bfloat16)
    grad_query = jnp.einsum(
        "hts,shd->thd", grad_scores, key_heads, preferred_element_type=jnp.float32
    )
    grad_key = jnp.einsum(
        "hts,thd->shd", grad_scores, query_heads, preferred_element_type=jnp.float32
    )
    return (
        grad_query.reshape(query_count, head_count * HD),
        grad_key.reshape(key_count, head_count * HD),
        grad_value.reshape(key_count, head_count * HD),
    )


def block_terms(
    query_rows,
    grad_rows,
    log_total,
    delta_rows,
    key_rows,
    value_rows,
    visible,
    head_count,
    score_scale,
):
    return pair_gradients(
        query_rows,
        grad_rows,
        log_total,
        delta_rows,
        key_rows,
        value_rows,
        visible,
        head_count,
        score_scale,
    )


def shards(queries, keys, values, saved_out, d_layer, out_weight, prefix, block_order):
    tok_rows = queries.shape[0]
    width = queries.shape[1]
    head_count = width // HD
    block_rows = tok_rows // 2
    blk_count = lax.axis_size("blk")
    blk_index = lax.axis_index("blk")
    score_scale = HD ** (-0.5)
    prefix_len = prefix[0]
    own_positions = row_positions(block_order, blk_index * tok_rows, tok_rows, block_rows)
    grad_out = jnp.einsum(
        "td,ed->te",
        lax.all_gather(d_layer, "head", axis=1, tiled=True),
        out_weight,
        preferred_element_type=jnp.float32,
    ).astype(jnp.bfloat16)
    query_heads = queries.reshape(tok_rows, head_count, HD)
    incoming = lax.all_gather(keys, "blk", axis=0, tiled=True)
    running_max = jnp.full((head_count, tok_rows), score_floor, jnp.float32)
    key_pos = row_positions(block_order, jnp.int32(0), incoming.shape[0], block_rows)
    visible = visible_pairs(own_positions, key_pos, prefix_len)
    key_heads = incoming.reshape(incoming.shape[0], head_count, HD)
    scores = (
        jnp.einsum("thd,shd->hts", query_heads, key_heads, preferred_element_type=jnp.float32)
        * score_scale
    )
    scores = jnp.where(visible[None], scores, score_floor)
    new_max = jnp.maximum(running_max, jnp.max(scores, axis=2))
    weights = jnp.where(visible[None], jnp.exp(scores - new_max[:, :, None]), 0.0)
    row_total = jnp.sum(weights, axis=2)
    log_total = new_max + jnp.log(row_total)
    products = grad_out.reshape(tok_rows, head_count, HD).astype(jnp.float32) * saved_out.reshape(
        tok_rows, head_count, HD
    ).astype(jnp.float32)
    delta_rows = jnp.sum(products, axis=2).T
    zeros_grad = jnp.zeros((tok_rows, width), jnp.float32)

    def key_turn(turn_index, state_now):
        key_rows, value_rows, grad_key, grad_value, grad_query = state_now
        anchor = (blk_index - turn_index) % blk_count
        key_pos = row_positions(block_order, anchor * tok_rows, tok_rows, block_rows)
        terms = block_terms(
            queries,
            grad_out,
            log_total,
            delta_rows,
            key_rows,
            value_rows,
            visible_pairs(own_positions, key_pos, prefix_len),
            head_count,
            score_scale,
        )
        key_rows, value_rows = shifted((key_rows, value_rows), "blk", 1)
        grad_key, grad_value = shifted((grad_key + terms[1], grad_value + terms[2]), "blk", 1)
        return (key_rows, value_rows, grad_key, grad_value, grad_query + terms[0])

    key_rows, value_rows, grad_key, grad_value, grad_query = lax.fori_loop(
        0, blk_count - 1, key_turn, (keys, values, zeros_grad, zeros_grad, zeros_grad)
    )
    anchor = (blk_index + 1) % blk_count
    key_pos = row_positions(block_order, anchor * tok_rows, tok_rows, block_rows)
    terms = block_terms(
        queries,
        grad_out,
        log_total,
        delta_rows,
        key_rows,
        value_rows,
        visible_pairs(own_positions, key_pos, prefix_len),
        head_count,
        score_scale,
    )
    grad_key, grad_value = (
        shifted((grad_key + terms[1]).astype(jnp.bfloat16), "blk", 1).astype(jnp.float32),
        shifted((grad_value + terms[2]).astype(jnp.bfloat16), "blk", 1).astype(jnp.float32),
    )
    grad_query = grad_query + terms[0]
    return (
        grad_query.astype(jnp.bfloat16),
        grad_key.astype(jnp.bfloat16),
        grad_value.astype(jnp.bfloat16),
    )


def solution(mesh):
    placed = (
        P("blk", "head"),
        P("blk", "head"),
        P("blk", "head"),
        P("blk", "head"),
        P("blk", "head"),
        P("head", None),
        P(),
        P(),
    )
    return jax.shard_map(
        shards,
        mesh=mesh,
        in_specs=placed,
        out_specs=(P("blk", "head"), P("blk", "head"), P("blk", "head")),
        check_vma=False,
    )
```

profile of v0, /device:TPU:1, one launch (start us, length us, event | category | flops | bytes accessed | tf_op | source)
XLA Modules:
  0.0 652.1 jit_solution(16534580675711777858)
XLA Ops:
  12.1 62.7 %all-gather.5.cloned.1.call-done = bf16[128,4096]{1,0:T(8,128)(2,1)} async-done(((bf16[128,256]{1,0:T(8,128)(2,1)}), bf16[128,4096]{1,0:T(8,128)(2,1)}) %all-gather.5.cloned.1.call-update) | async-done | bytes 1048592 | tf_op jit(solution)/shard_map/all_gather | solution.py:109
  76.9 68.5 %all-gather.3.cloned.1.call-done = bf16[4096,256]{1,0:T(8,128)(2,1)} async-done(((bf16[128,256]{1,0:T(8,128)(2,1)}), bf16[4096,256]{1,0:T(8,128)(2,1)}) %all-gather.3.cloned.1.call-update) | async-done | bytes 2097168 | tf_op jit(solution)/shard_map/all_gather | solution.py:114
  148.8 486.9 %while.25 = (s32[]{:T(128)}, bf16[128,256]{1,0:T(8,128)(2,1)S(1)}, bf16[128,256]{1,0:T(8,128)(2,1)S(1)}, f32[128,256]{1,0:T(8,128)S(1)}, f32[128,256]{1,0:T(8,12...) while((s32[]{:T(128)}, bf16[128,256]{1,0:T(8,128)(2,1)S(1)}, ...), condition=%wide.region_7.8_spmd.clone, body=%wide.region_5.7_spmd.clone.sunk | while | flops 42282768 | bytes 3380712 | solution.py:153
  162.4 4.3 collective-permute-start
  178.4 4.3 collective-permute-start
  194.1 4.3 collective-permute-start
  224.6 4.3 collective-permute-start
  232.2 4.4 collective-permute-start.2
  240.6 4.3 collective-permute-start
  248.3 4.7 collective-permute-start.2
  257.0 4.3 collective-permute-start
  264.6 5.3 collective-permute-start.2
  274.0 4.3 collective-permute-start
  289.7 4.3 collective-permute-start
  321.1 4.3 collective-permute-start
  336.9 4.3 collective-permute-start
  352.6 4.3 collective-permute-start
  368.3 4.3 collective-permute-start
  384.1 4.3 collective-permute-start
  399.8 4.3 collective-permute-start
  415.5 4.3 collective-permute-start
  431.3 4.3 collective-permute-start
  447.0 4.3 collective-permute-start
  636.2 4.4 collective-permute-start.5
  (582 shorter events, 409.7 us)
Async XLA Ops:
  7.2 67.5 %all-gather.5.cloned.1.call-start = ((), (), s32[]{:S(2)}) async-start(), calls=%async_computation.1 | async-start | bytes 1114112 | tf_op jit(solution)/shard_map/all_gather | solution.py:109
  8.9 136.5 %all-gather.3.cloned.1.call-start = ((), (), s32[]{:S(2)}) async-start(), calls=%async_computation | async-start | bytes 2162688 | tf_op jit(solution)/shard_map/all_gather | solution.py:114
  162.4 14.3 %collective-permute-start = (bf16[128,256]{1,0:T(8,128)(2,1)S(1)}, bf16[128,256]{1,0:T(8,128)(2,1)S(1)}, u32[]{:S(2)}, u32[]{:S(2)}) collective-permute-start(bf16[128,256]{1,0:T(8,128)(2,1)S(1)} %copy.31), channel_id=1, source_target_pairs={{0,16},{16,32},{32,48},{48,64},{64,80},{80,96},{96,112},{112,128},... | collective-permute-start | bytes 196616 | tf_op jit(solution)/shard_map/while/body/eval_jaxpr/ppermute | solution.py:15
  178.4 14.0 %collective-permute-start = (bf16[128,256]{1,0:T(8,128)(2,1)S(1)}, bf16[128,256]{1,0:T(8,128)(2,1)S(1)}, u32[]{:S(2)}, u32[]{:S(2)}) collective-permute-start(bf16[128,256]{1,0:T(8,128)(2,1)S(1)} %copy.31), channel_id=1, source_target_pairs={{0,16},{16,32},{32,48},{48,64},{64,80},{80,96},{96,112},{112,128},... | collective-permute-start | bytes 196616 | tf_op jit(solution)/shard_map/while/body/eval_jaxpr/ppermute | solution.py:15
  194.1 14.2 %collective-permute-start = (bf16[128,256]{1,0:T(8,128)(2,1)S(1)}, bf16[128,256]{1,0:T(8,128)(2,1)S(1)}, u32[]{:S(2)}, u32[]{:S(2)}) collective-permute-start(bf16[128,256]{1,0:T(8,128)(2,1)S(1)} %copy.31), channel_id=1, source_target_pairs={{0,16},{16,32},{32,48},{48,64},{64,80},{80,96},{96,112},{112,128},... | collective-permute-start | bytes 196616 | tf_op jit(solution)/shard_map/while/body/eval_jaxpr/ppermute | solution.py:15
  224.6 14.3 %collective-permute-start = (bf16[128,256]{1,0:T(8,128)(2,1)S(1)}, bf16[128,256]{1,0:T(8,128)(2,1)S(1)}, u32[]{:S(2)}, u32[]{:S(2)}) collective-permute-start(bf16[128,256]{1,0:T(8,128)(2,1)S(1)} %copy.31), channel_id=1, source_target_pairs={{0,16},{16,32},{32,48},{48,64},{64,80},{80,96},{96,112},{112,128},... | collective-permute-start | bytes 196616 | tf_op jit(solution)/shard_map/while/body/eval_jaxpr/ppermute | solution.py:15
  240.6 14.6 %collective-permute-start = (bf16[128,256]{1,0:T(8,128)(2,1)S(1)}, bf16[128,256]{1,0:T(8,128)(2,1)S(1)}, u32[]{:S(2)}, u32[]{:S(2)}) collective-permute-start(bf16[128,256]{1,0:T(8,128)(2,1)S(1)} %copy.31), channel_id=1, source_target_pairs={{0,16},{16,32},{32,48},{48,64},{64,80},{80,96},{96,112},{112,128},... | collective-permute-start | bytes 196616 | tf_op jit(solution)/shard_map/while/body/eval_jaxpr/ppermute | solution.py:15
  257.0 15.2 %collective-permute-start = (bf16[128,256]{1,0:T(8,128)(2,1)S(1)}, bf16[128,256]{1,0:T(8,128)(2,1)S(1)}, u32[]{:S(2)}, u32[]{:S(2)}) collective-permute-start(bf16[128,256]{1,0:T(8,128)(2,1)S(1)} %copy.31), channel_id=1, source_target_pairs={{0,16},{16,32},{32,48},{48,64},{64,80},{80,96},{96,112},{112,128},... | collective-permute-start | bytes 196616 | tf_op jit(solution)/shard_map/while/body/eval_jaxpr/ppermute | solution.py:15
  289.7 14.0 %collective-permute-start = (bf16[128,256]{1,0:T(8,128)(2,1)S(1)}, bf16[128,256]{1,0:T(8,128)(2,1)S(1)}, u32[]{:S(2)}, u32[]{:S(2)}) collective-permute-start(bf16[128,256]{1,0:T(8,128)(2,1)S(1)} %copy.31), channel_id=1, source_target_pairs={{0,16},{16,32},{32,48},{48,64},{64,80},{80,96},{96,112},{112,128},... | collective-permute-start | bytes 196616 | tf_op jit(solution)/shard_map/while/body/eval_jaxpr/ppermute | solution.py:15
  305.4 14.0 %collective-permute-start = (bf16[128,256]{1,0:T(8,128)(2,1)S(1)}, bf16[128,256]{1,0:T(8,128)(2,1)S(1)}, u32[]{:S(2)}, u32[]{:S(2)}) collective-permute-start(bf16[128,256]{1,0:T(8,128)(2,1)S(1)} %copy.31), channel_id=1, source_target_pairs={{0,16},{16,32},{32,48},{48,64},{64,80},{80,96},{96,112},{112,128},... | collective-permute-start | bytes 196616 | tf_op jit(solution)/shard_map/while/body/eval_jaxpr/ppermute | solution.py:15
  321.1 14.0 %collective-permute-start = (bf16[128,256]{1,0:T(8,128)(2,1)S(1)}, bf16[128,256]{1,0:T(8,128)(2,1)S(1)}, u32[]{:S(2)}, u32[]{:S(2)}) collective-permute-start(bf16[128,256]{1,0:T(8,128)(2,1)S(1)} %copy.31), channel_id=1, source_target_pairs={{0,16},{16,32},{32,48},{48,64},{64,80},{80,96},{96,112},{112,128},... | collective-permute-start | bytes 196616 | tf_op jit(solution)/shard_map/while/body/eval_jaxpr/ppermute | solution.py:15
  336.9 14.0 %collective-permute-start = (bf16[128,256]{1,0:T(8,128)(2,1)S(1)}, bf16[128,256]{1,0:T(8,128)(2,1)S(1)}, u32[]{:S(2)}, u32[]{:S(2)}) collective-permute-start(bf16[128,256]{1,0:T(8,128)(2,1)S(1)} %copy.31), channel_id=1, source_target_pairs={{0,16},{16,32},{32,48},{48,64},{64,80},{80,96},{96,112},{112,128},... | collective-permute-start | bytes 196616 | tf_op jit(solution)/shard_map/while/body/eval_jaxpr/ppermute | solution.py:15
  352.6 14.0 %collective-permute-start = (bf16[128,256]{1,0:T(8,128)(2,1)S(1)}, bf16[128,256]{1,0:T(8,128)(2,1)S(1)}, u32[]{:S(2)}, u32[]{:S(2)}) collective-permute-start(bf16[128,256]{1,0:T(8,128)(2,1)S(1)} %copy.31), channel_id=1, source_target_pairs={{0,16},{16,32},{32,48},{48,64},{64,80},{80,96},{96,112},{112,128},... | collective-permute-start | bytes 196616 | tf_op jit(solution)/shard_map/while/body/eval_jaxpr/ppermute | solution.py:15
  368.3 14.0 %collective-permute-start = (bf16[128,256]{1,0:T(8,128)(2,1)S(1)}, bf16[128,256]{1,0:T(8,128)(2,1)S(1)}, u32[]{:S(2)}, u32[]{:S(2)}) collective-permute-start(bf16[128,256]{1,0:T(8,128)(2,1)S(1)} %copy.31), channel_id=1, source_target_pairs={{0,16},{16,32},{32,48},{48,64},{64,80},{80,96},{96,112},{112,128},... | collective-permute-start | bytes 196616 | tf_op jit(solution)/shard_map/while/body/eval_jaxpr/ppermute | solution.py:15
  384.1 14.0 %collective-permute-start = (bf16[128,256]{1,0:T(8,128)(2,1)S(1)}, bf16[128,256]{1,0:T(8,128)(2,1)S(1)}, u32[]{:S(2)}, u32[]{:S(2)}) collective-permute-start(bf16[128,256]{1,0:T(8,128)(2,1)S(1)} %copy.31), channel_id=1, source_target_pairs={{0,16},{16,32},{32,48},{48,64},{64,80},{80,96},{96,112},{112,128},... | collective-permute-start | bytes 196616 | tf_op jit(solution)/shard_map/while/body/eval_jaxpr/ppermute | solution.py:15
  399.8 14.0 %collective-permute-start = (bf16[128,256]{1,0:T(8,128)(2,1)S(1)}, bf16[128,256]{1,0:T(8,128)(2,1)S(1)}, u32[]{:S(2)}, u32[]{:S(2)}) collective-permute-start(bf16[128,256]{1,0:T(8,128)(2,1)S(1)} %copy.31), channel_id=1, source_target_pairs={{0,16},{16,32},{32,48},{48,64},{64,80},{80,96},{96,112},{112,128},... | collective-permute-start | bytes 196616 | tf_op jit(solution)/shard_map/while/body/eval_jaxpr/ppermute | solution.py:15
  415.5 14.0 %collective-permute-start = (bf16[128,256]{1,0:T(8,128)(2,1)S(1)}, bf16[128,256]{1,0:T(8,128)(2,1)S(1)}, u32[]{:S(2)}, u32[]{:S(2)}) collective-permute-start(bf16[128,256]{1,0:T(8,128)(2,1)S(1)} %copy.31), channel_id=1, source_target_pairs={{0,16},{16,32},{32,48},{48,64},{64,80},{80,96},{96,112},{112,128},... | collective-permute-start | bytes 196616 | tf_op jit(solution)/shard_map/while/body/eval_jaxpr/ppermute | solution.py:15
  431.3 14.0 %collective-permute-start = (bf16[128,256]{1,0:T(8,128)(2,1)S(1)}, bf16[128,256]{1,0:T(8,128)(2,1)S(1)}, u32[]{:S(2)}, u32[]{:S(2)}) collective-permute-start(bf16[128,256]{1,0:T(8,128)(2,1)S(1)} %copy.31), channel_id=1, source_target_pairs={{0,16},{16,32},{32,48},{48,64},{64,80},{80,96},{96,112},{112,128},... | collective-permute-start | bytes 196616 | tf_op jit(solution)/shard_map/while/body/eval_jaxpr/ppermute | solution.py:15
  447.0 14.0 %collective-permute-start = (bf16[128,256]{1,0:T(8,128)(2,1)S(1)}, bf16[128,256]{1,0:T(8,128)(2,1)S(1)}, u32[]{:S(2)}, u32[]{:S(2)}) collective-permute-start(bf16[128,256]{1,0:T(8,128)(2,1)S(1)} %copy.31), channel_id=1, source_target_pairs={{0,16},{16,32},{32,48},{48,64},{64,80},{80,96},{96,112},{112,128},... | collective-permute-start | bytes 196616 | tf_op jit(solution)/shard_map/while/body/eval_jaxpr/ppermute | solution.py:15
  462.7 14.0 %collective-permute-start = (bf16[128,256]{1,0:T(8,128)(2,1)S(1)}, bf16[128,256]{1,0:T(8,128)(2,1)S(1)}, u32[]{:S(2)}, u32[]{:S(2)}) collective-permute-start(bf16[128,256]{1,0:T(8,128)(2,1)S(1)} %copy.31), channel_id=1, source_target_pairs={{0,16},{16,32},{32,48},{48,64},{64,80},{80,96},{96,112},{112,128},... | collective-permute-start | bytes 196616 | tf_op jit(solution)/shard_map/while/body/eval_jaxpr/ppermute | solution.py:15
  478.5 14.0 %collective-permute-start = (bf16[128,256]{1,0:T(8,128)(2,1)S(1)}, bf16[128,256]{1,0:T(8,128)(2,1)S(1)}, u32[]{:S(2)}, u32[]{:S(2)}) collective-permute-start(bf16[128,256]{1,0:T(8,128)(2,1)S(1)} %copy.31), channel_id=1, source_target_pairs={{0,16},{16,32},{32,48},{48,64},{64,80},{80,96},{96,112},{112,128},... | collective-permute-start | bytes 196616 | tf_op jit(solution)/shard_map/while/body/eval_jaxpr/ppermute | solution.py:15
  494.2 14.0 %collective-permute-start = (bf16[128,256]{1,0:T(8,128)(2,1)S(1)}, bf16[128,256]{1,0:T(8,128)(2,1)S(1)}, u32[]{:S(2)}, u32[]{:S(2)}) collective-permute-start(bf16[128,256]{1,0:T(8,128)(2,1)S(1)} %copy.31), channel_id=1, source_target_pairs={{0,16},{16,32},{32,48},{48,64},{64,80},{80,96},{96,112},{112,128},... | collective-permute-start | bytes 196616 | tf_op jit(solution)/shard_map/while/body/eval_jaxpr/ppermute | solution.py:15
  509.9 14.0 %collective-permute-start = (bf16[128,256]{1,0:T(8,128)(2,1)S(1)}, bf16[128,256]{1,0:T(8,128)(2,1)S(1)}, u32[]{:S(2)}, u32[]{:S(2)}) collective-permute-start(bf16[128,256]{1,0:T(8,128)(2,1)S(1)} %copy.31), channel_id=1, source_target_pairs={{0,16},{16,32},{32,48},{48,64},{64,80},{80,96},{96,112},{112,128},... | collective-permute-start | bytes 196616 | tf_op jit(solution)/shard_map/while/body/eval_jaxpr/ppermute | solution.py:15
  541.4 14.0 %collective-permute-start = (bf16[128,256]{1,0:T(8,128)(2,1)S(1)}, bf16[128,256]{1,0:T(8,128)(2,1)S(1)}, u32[]{:S(2)}, u32[]{:S(2)}) collective-permute-start(bf16[128,256]{1,0:T(8,128)(2,1)S(1)} %copy.31), channel_id=1, source_target_pairs={{0,16},{16,32},{32,48},{48,64},{64,80},{80,96},{96,112},{112,128},... | collective-permute-start | bytes 196616 | tf_op jit(solution)/shard_map/while/body/eval_jaxpr/ppermute | solution.py:15
  (109 other events, 959.5 us)
Sparse Core Ops, SparseCore 0:
  11.0 63.6 all-gather.4
  77.4 67.8 all-gather.2
where the time goes:
time: 659 us; the launch traced here: 652 us
  starting transfers between devices  384 us (58%)
  waiting for transfers between devices  185 us (28%)
  matrix products  33.5 us (5%)
  other arithmetic  26.2 us (4%)
  between operations  14.9 us (2%)
    ppermute x126, starting transfers between devices, shifted(): return lax.ppermute(value, axis, pairs)  384 us
    all_gather x1, waiting for transfers between devices, shards(): incoming = lax.all_gather(keys, 'blk', axis=0, tiled=True)  68.5 us
    all_gather x1, waiting for transfers between devices, shards(): lax.all_gather(d_layer, 'head', axis=1, tiled=True)  62.7 us
    ppermute x126, waiting for transfers between devices, shifted(): return lax.ppermute(value, axis, pairs)  53.4 us
    lt x33, other arithmetic, visible_pairs(): key_pos[None, :] < prefix_len  20.5 us
  transfers between devices with their start and end apart: 128, of which 33 were waited for; matrix products, arithmetic and copies ran while one was open for 9% of the time, Pallas kernels for 0%

commit v1 on v0

v1 whole, which is shorter than its diff:
```python
import functools

import jax
import jax.numpy as jnp
from jax import lax
from jax.experimental import pallas as pl
from jax.experimental.pallas import tpu as pltpu
from jax.sharding import PartitionSpec as P

MESH = pl.DeviceIdType.MESH
F32 = jnp.float32
BF16 = jnp.bfloat16

HD = 256
ROWS = 128
HALF = ROWS // 2
NZ = 8
NJ = 4
NH = 4
FLOOR = -1e30
SCALE = HD ** -0.5
MESSAGES = 63


def nt(a, b):
    return lax.dot_general(a, b, (((1,), (1,)), ((), ())), preferred_element_type=F32)


def nn(a, b):
    return lax.dot_general(a, b, (((1,), (0,)), ((), ())), preferred_element_type=F32)


def tn(a, b):
    return lax.dot_general(a, b, (((0,), (0,)), ((), ())), preferred_element_type=F32)


def rows(slot, count=ROWS, first=0):
    return pl.ds(slot * ROWS + first, count)


def kernel(
    prefix_ref,
    order_ref,
    q_hbm,
    k_hbm,
    v_hbm,
    o_hbm,
    d_hbm,
    w_hbm,
    dq_out,
    dk_out,
    dv_out,
    qb,
    kb,
    vb,
    ob,
    dl,
    wb,
    gb,
    st,
    delta,
    score,
    prob,
    ds,
    dv_acc,
    dk_acc,
    dq_acc,
    dv_send,
    dk_send,
    dv_recv,
    dk_recv,
    dq_send,
    dq_recv,
    local_sem,
    send_sem,
    recv_sem,
):
    blk = lax.axis_index("blk")
    head = lax.axis_index("head")
    z, j = lax.div(blk, NJ), lax.rem(blk, NJ)
    yh, x = lax.div(head, NH), lax.rem(head, NH)

    def at_z(step):
        return (lax.rem(z + (step + NZ), NZ) * NJ + j, head)

    def at_y(step):
        return (blk, lax.rem(yh + (step + NH), NH) * NH + x)

    def at_x(step):
        return (blk, yh * NH + lax.rem(x + (step + NH), NH))

    core_peer = (z * NJ + j + 1 - 2 * lax.rem(j, 2), head)
    pair_peer = (z * NJ + j + 2 - 4 * lax.div(j, 2), head)

    loads = {}

    def load(name, src, dst):
        copy = pltpu.make_async_copy(src, dst, local_sem.at[len(loads)])
        copy.start()
        loads[name] = copy

    load("k", k_hbm, kb.at[rows(0)])
    load("q", q_hbm, qb.at[rows(0)])
    load("d", d_hbm, dl.at[rows(0)])
    load("v", v_hbm, vb.at[rows(0)])
    load("w", w_hbm, wb)
    load("o", o_hbm, ob)

    barrier = pltpu.get_barrier_semaphore()
    neighbours = (at_z(1), at_z(-1), at_y(1), at_y(-1), at_x(1), at_x(-1), core_peer, pair_peer)
    for device in neighbours:
        pl.semaphore_signal(barrier, inc=1, device_id=device, device_id_type=MESH)
    pl.semaphore_wait(barrier, len(neighbours))

    sent = {}

    def send(name, src, dst, device):
        index = len(sent)
        copy = pltpu.make_async_remote_copy(
            src_ref=src,
            dst_ref=dst,
            send_sem=send_sem.at[index],
            recv_sem=recv_sem.at[index],
            device_id=device,
            device_id_type=MESH,
        )
        copy.start()
        sent[name] = copy

    def arrived(*names):
        for name in names:
            sent[name].wait_recv()

    def slot_of(dy, dx):
        return (dy % NH) * NH + dx % NH

    def x_start(dy):
        src = dl.at[rows(slot_of(dy, 0))] if dy else d_hbm
        send(("x+", dy), src, dl.at[rows(slot_of(dy, -1))], at_x(1))
        send(("x-", dy), src, dl.at[rows(slot_of(dy, 1))], at_x(-1))

    def x_relay(dy):
        arrived(("x+", dy))
        low = rows(slot_of(dy, -1), HALF)
        send(("xh+", dy), dl.at[low], dl.at[rows(slot_of(dy, 2), HALF)], at_x(1))
        arrived(("x-", dy))
        high = rows(slot_of(dy, 1), HALF, HALF)
        send(("xh-", dy), dl.at[high], dl.at[rows(slot_of(dy, 2), HALF, HALF)], at_x(-1))

    def z_step(kind, hbm, buf, step):
        if step == 0:
            up, down = hbm, hbm
        else:
            arrived((kind, "+", step - 1), (kind, "-", step - 1))
            up, down = buf.at[rows(NZ - step)], buf.at[rows(step)]
        if step < 3:
            send((kind, "+", step), up, buf.at[rows(NZ - 1 - step)], at_z(1))
            send((kind, "-", step), down, buf.at[rows(step + 1)], at_z(-1))
        else:
            low, high = rows(NZ - 3, HALF), rows(3, HALF, HALF)
            send((kind, "+", step), buf.at[low], buf.at[rows(4, HALF)], at_z(1))
            send((kind, "-", step), buf.at[high], buf.at[rows(4, HALF, HALF)], at_z(-1))

    send("y+", d_hbm, dl.at[rows(slot_of(-1, 0))], at_y(1))
    send("y-", d_hbm, dl.at[rows(slot_of(1, 0))], at_y(-1))
    z_step("k", k_hbm, kb, 0)
    x_start(0)
    send("q core", q_hbm, qb.at[rows(1)], core_peer)
    send("q pair", q_hbm, qb.at[rows(2)], pair_peer)
    z_step("v", v_hbm, vb, 0)

    lane = lax.broadcasted_iota(jnp.int32, (1, ROWS), 1)
    sub = lax.broadcasted_iota(jnp.int32, (ROWS, 1), 0)

    def block_positions(index, iota):
        first, second = order_ref[2 * index], order_ref[2 * index + 1]
        return jnp.where(iota < HALF, first * HALF + iota, second * HALF + iota - HALF)

    group = (
        blk,
        z * NJ + j + 1 - 2 * lax.rem(j, 2),
        z * NJ + j + 2 - 4 * lax.div(j, 2),
        z * NJ + 3 - j,
    )
    reach = jnp.concatenate([block_positions(member, lane) for member in group], axis=1)
    reach = jnp.maximum(reach, prefix_ref[0] - 1)

    def score_block(dz):
        scores = nt(kb[rows(dz)], qb[...]) * SCALE
        key_pos = block_positions(lax.rem(z + dz, NZ) * NJ + j, sub)
        scores = jnp.where(key_pos <= reach, scores, FLOOR)
        score[rows(dz)] = scores
        return jnp.max(scores, axis=0, keepdims=True)

    def project(slots):
        total = None
        for dy, dx in slots:
            source = lax.rem(yh + dy % NH, NH) * NH + lax.rem(x + dx % NH, NH)
            columns = pl.ds(pl.multiple_of(source * HD, HD), HD)
            term = nt(dl[rows(slot_of(dy, dx))], wb[:, columns])
            total = term if total is None else total + term
        return total

    x_relay(0)
    z_step("k", k_hbm, kb, 1)
    arrived("q pair")
    send("q on", qb.at[rows(2)], qb.at[rows(3)], core_peer)
    arrived("y+")
    send("yh+", dl.at[rows(slot_of(-1, 0), HALF)], dl.at[rows(slot_of(2, 0), HALF)], at_y(1))
    x_start(3)
    arrived("y-")
    send("yh-", dl.at[rows(slot_of(1, 0), HALF, HALF)], dl.at[rows(slot_of(2, 0), HALF, HALF)], at_y(-1))
    x_start(1)
    z_step("v", v_hbm, vb, 1)
    loads["q"].wait()
    loads["k"].wait()
    arrived("q core", "q on")
    top = score_block(0)
    z_step("k", k_hbm, kb, 2)
    top = jnp.maximum(top, score_block(1))
    top = jnp.maximum(top, score_block(7))
    z_step("v", v_hbm, vb, 2)
    x_relay(3)
    x_relay(1)
    arrived("yh+", "yh-")
    x_start(2)
    z_step("k", k_hbm, kb, 3)
    loads["w"].wait()
    loads["d"].wait()
    arrived(("xh+", 0), ("xh-", 0))
    grad = project([(0, 0), (0, 1), (0, 3), (0, 2)])
    top = jnp.maximum(top, score_block(2))
    top = jnp.maximum(top, score_block(6))
    z_step("v", v_hbm, vb, 3)
    top = jnp.maximum(top, score_block(3))
    top = jnp.maximum(top, score_block(5))
    grad = grad + project([(1, 0), (1, 1), (1, 3), (3, 0), (3, 1), (3, 3)])
    x_relay(2)
    arrived(("k", "+", 3), ("k", "-", 3))
    top = jnp.maximum(top, score_block(4))

    def chunk_sum(dz, total):
        return total + jnp.sum(jnp.exp(score[pl.ds(pl.multiple_of(dz * ROWS, ROWS), ROWS)] - top), axis=0, keepdims=True)

    total = lax.fori_loop(0, NZ, chunk_sum, jnp.zeros((1, NJ * ROWS), F32))

    def swapped(row, distance):
        parts = [row[:, (member ^ distance) * ROWS:((member ^ distance) + 1) * ROWS] for member in range(NJ)]
        return jnp.concatenate(parts, axis=1)

    def exchange(step, name, device, distance, top, total):
        st[2 * step] = jnp.concatenate([jnp.broadcast_to(top, (4, NJ * ROWS)), jnp.broadcast_to(total, (4, NJ * ROWS))], axis=0)
        send(name, st.at[2 * step], st.at[2 * step + 1], device)
        return lambda: merge(step, name, distance, top, total)

    def merge(step, name, distance, top, total):
        arrived(name)
        other_top = swapped(st[2 * step + 1, 0:1], distance)
        other_total = swapped(st[2 * step + 1, 4:5], distance)
        new_top = jnp.maximum(top, other_top)
        return new_top, total * jnp.exp(top - new_top) + other_total * jnp.exp(other_top - new_top)

    finish = exchange(0, "s core", core_peer, 1, top, total)
    arrived(("xh+", 1), ("xh-", 1), ("xh+", 3), ("xh-", 3))
    grad = grad + project([(1, 2), (3, 2), (2, 0), (2, 1), (2, 3)])
    top, total = finish()
    finish = exchange(1, "s pair", pair_peer, 2, top, total)
    loads["o"].wait()

    arrived(("xh+", 2), ("xh-", 2))
    grad = grad + project([(2, 2)])
    grad_low = grad.astype(BF16)
    gb[rows(0)] = grad_low
    send("g core", gb.at[rows(0)], gb.at[rows(1)], core_peer)
    send("g pair", gb.at[rows(0)], gb.at[rows(2)], pair_peer)
    products = grad_low.astype(F32) * ob[...].astype(F32)
    ones = jnp.ones((8, HD), F32)
    delta[0] = lax.dot_general(
        ones, products, (((1,), (1,)), ((), ())), precision=lax.Precision.HIGHEST, preferred_element_type=F32
    )
    send("t core", delta.at[0], delta.at[1], core_peer)
    send("t pair", delta.at[0], delta.at[2], pair_peer)

    top, total = finish()
    log_total = top + jnp.log(total)

    def make_prob(dz, carry):
        here = pl.ds(pl.multiple_of(dz * ROWS, ROWS), ROWS)
        probs = jnp.exp(score[here] - log_total)
        score[here] = probs
        prob[here] = probs.astype(BF16)
        return carry

    lax.fori_loop(0, NZ, make_prob, 0)
    arrived(("v", "+", 3), ("v", "-", 3))
    loads["v"].wait()

    def pair_terms(pair, here, delta_row):
        columns = pl.ds(2 * ROWS * pair, 2 * ROWS)
        grad_pair = gb[columns]
        grad_probs = nt(vb[here], grad_pair)
        grad_scores = (score[here, columns] * (grad_probs - delta_row) * SCALE).astype(BF16)
        ds[here, columns] = grad_scores
        return nn(prob[here, columns], grad_pair), nn(grad_scores, qb[columns])

    arrived("g core", "t core")
    delta_row = jnp.concatenate([delta[0, 0:1], delta[1, 0:1]], axis=1)

    def first_pair(dz, carry):
        here = pl.ds(pl.multiple_of(dz * ROWS, ROWS), ROWS)
        dv, dk = pair_terms(0, here, delta_row)
        dv_acc[here] = dv
        dk_acc[here] = dk
        return carry

    arrived("g pair")
    send("g on", gb.at[rows(2)], gb.at[rows(3)], core_peer)
    arrived("t pair")
    send("t on", delta.at[2], delta.at[3], core_peer)
    lax.fori_loop(0, NZ, first_pair, 0)
    arrived("g on", "t on")
    delta_far = jnp.concatenate([delta[2, 0:1], delta[3, 0:1]], axis=1)

    def second_pair(dz):
        here = rows(dz)
        dv, dk = pair_terms(1, here, delta_far)
        dv_acc[here] = dv_acc[here] + dv
        dk_acc[here] = dk_acc[here] + dk

    def pass_on(kind, acc, out, recv, dz, way, first):
        value = acc[rows(dz)]
        if not first:
            arrived((kind, way, dz))
            value = value + recv[rows(dz)].astype(F32)
        out[rows(dz)] = value.astype(BF16)
        target = (dz - way) % NZ
        landing = target
        if target == 0 and (dz, way) == (1, 1) and kind == "dv":
            landing = 4
        if target == 0 and (dz, way) == (7, -1) and kind == "dk":
            landing = 4
        send((kind, way, target), out.at[rows(dz)], recv.at[rows(landing)], at_z(way))

    dv_pass = functools.partial(pass_on, "dv", dv_acc, dv_send, dv_recv)
    dk_pass = functools.partial(pass_on, "dk", dk_acc, dk_send, dk_recv)

    second_pair(4)
    dv_pass(4, -1, True)
    dk_pass(4, 1, True)
    second_pair(3)
    dv_pass(3, 1, True)
    second_pair(5)
    dk_pass(5, -1, True)
    dv_pass(5, -1, False)
    dk_pass(3, 1, False)
    second_pair(2)
    second_pair(6)
    dv_pass(2, 1, False)
    dk_pass(6, -1, False)
    dv_pass(6, -1, False)
    dk_pass(2, 1, False)
    second_pair(1)
    second_pair(7)
    second_pair(0)
    dv_pass(1, 1, False)
    dk_pass(7, -1, False)
    dv_pass(7, -1, False)
    dk_pass(1, 1, False)

    dq = tn(ds[:, 2 * ROWS:], kb[...])
    dq_send[0:2 * ROWS] = dq.astype(BF16)
    send("dq pair", dq_send.at[pl.ds(0, 2 * ROWS)], dq_recv.at[pl.ds(0, 2 * ROWS)], pair_peer)
    dq_acc[...] = tn(ds[:, :2 * ROWS], kb[...])
    arrived("dq pair")
    dq_send[rows(2)] = (dq_acc[rows(1)] + dq_recv[rows(1)].astype(F32)).astype(BF16)
    send("dq core", dq_send.at[rows(2)], dq_recv.at[rows(2)], core_peer)
    dq = dq_acc[rows(0)] + dq_recv[rows(0)].astype(F32)
    arrived("dq core")
    dq_out[...] = (dq + dq_recv[rows(2)].astype(F32)).astype(BF16)

    def own(kind, acc, recv):
        arrived((kind, 1, 0), (kind, -1, 0))
        return (acc[rows(0)] + recv[rows(0)].astype(F32) + recv[rows(4)].astype(F32)).astype(BF16)

    dv_out[...] = own("dv", dv_acc, dv_recv)
    dk_out[...] = own("dk", dk_acc, dk_recv)
    for copy in sent.values():
        copy.wait_send()


def shards(queries, keys, values, saved_out, d_layer, out_weight, prefix, block_order):
    block = jax.ShapeDtypeStruct((ROWS, HD), BF16)
    anywhere = pl.BlockSpec(memory_space=pl.ANY)
    scalars = pl.BlockSpec(memory_space=pltpu.SMEM)
    vmem = pl.BlockSpec(memory_space=pltpu.VMEM)
    return pl.pallas_call(
        kernel,
        out_shape=(block, block, block),
        in_specs=[scalars, scalars] + [anywhere] * 6,
        out_specs=(vmem, vmem, vmem),
        scratch_shapes=[
            pltpu.VMEM((NJ * ROWS, HD), BF16),
            pltpu.VMEM((NZ * ROWS, HD), BF16),
            pltpu.VMEM((NZ * ROWS, HD), BF16),
            pltpu.VMEM((ROWS, HD), BF16),
            pltpu.VMEM((NH * NH * ROWS, HD), BF16),
            pltpu.VMEM((HD, NH * NH * HD), BF16),
            pltpu.VMEM((NJ * ROWS, HD), BF16),
            pltpu.VMEM((4, 8, NJ * ROWS), F32),
            pltpu.VMEM((NJ, 8, ROWS), F32),
            pltpu.VMEM((NZ * ROWS, NJ * ROWS), F32),
            pltpu.VMEM((NZ * ROWS, NJ * ROWS), BF16),
            pltpu.VMEM((NZ * ROWS, NJ * ROWS), BF16),
            pltpu.VMEM((NZ * ROWS, HD), F32),
            pltpu.VMEM((NZ * ROWS, HD), F32),
            pltpu.VMEM((2 * ROWS, HD), F32),
            pltpu.VMEM((NZ * ROWS, HD), BF16),
            pltpu.VMEM((NZ * ROWS, HD), BF16),
            pltpu.VMEM((NZ * ROWS, HD), BF16),
            pltpu.VMEM((NZ * ROWS, HD), BF16),
            pltpu.VMEM((3 * ROWS, HD), BF16),
            pltpu.VMEM((3 * ROWS, HD), BF16),
            pltpu.SemaphoreType.DMA((6,)),
            pltpu.SemaphoreType.DMA((MESSAGES,)),
            pltpu.SemaphoreType.DMA((MESSAGES,)),
        ],
        compiler_params=pltpu.CompilerParams(
            collective_id=0, has_side_effects=True, vmem_limit_bytes=48 * 1024 * 1024
        ),
    )(prefix, block_order, queries, keys, values, saved_out, d_layer, out_weight)


def solution(mesh):
    tokens = P("blk", "head")
    return jax.shard_map(
        shards,
        mesh=mesh,
        in_specs=(tokens, tokens, tokens, tokens, tokens, P("head", None), P(), P()),
        out_specs=(tokens, tokens, tokens),
        check_vma=False,
    )
```

time: 659 us -> 69.6 us (0.11)
  starting transfers between devices: 384 us -> 0 us
  waiting for transfers between devices: 185 us -> 0 us
  Pallas kernels: 0 us -> 59.6 us
  matrix products: 33.5 us -> 0 us
  other arithmetic: 26.2 us -> 0 us
  between operations: 14.9 us -> 1.3 us
    ppermute x126 -> x0, starting transfers between devices: 384 us -> none  [shifted(): return lax.ppermute(value, axis, pairs)]
    all_gather x2 -> x0, waiting for transfers between devices: 131 us -> none  [the longest x1 68.5 us: shards(): incoming = lax.all_gather(keys, 'blk', axis=0, tiled=True)]
    pallas_call x0 -> x1, Pallas kernels: none -> 59.6 us  [shards(): pl.pallas_call(kernel, out_shape=(block, block, block), in_specs=[scalars...]
    ppermute x126 -> x0, waiting for transfers between devices: 53.4 us -> none  [shifted(): return lax.ppermute(value, axis, pairs)]
    dot_general x162 -> x0, matrix products: 33.5 us -> none  [the longest x32 6.36 us: pair_gradients(): jnp.einsum('hts,thd->shd', probs.astype(jnp.bfloat16), grad_heads, prefer...]
    lt x33 -> x0, other arithmetic: 20.5 us -> none  [visible_pairs(): key_pos[None, :] < prefix_len]
  transfers between devices with their start and end apart: 128 -> 0, of which waited for: 33 -> 0; matrix products, arithmetic and copies ran while one was open for 9% -> 0% of each run, Pallas kernels for 0% -> 0%
where the time goes in v1:
time: 69.6 us; the launch traced here: 69.2 us
  Pallas kernels  59.6 us (86%)
  local copies, waits for them, and re-layouts  8.32 us (12%)
  between operations  1.3 us (2%)
    pallas_call x1, Pallas kernels, shards(): pl.pallas_call(kernel, out_shape=(block, block, block), in_specs=[scalars...  59.6 us
    unnamed x17, local copies, waits for them, and re-layouts  8.32 us

profile of v1, /device:TPU:1, one launch (start us, length us, event | category | flops | bytes accessed | tf_op | source)
XLA Modules:
  0.0 69.2 jit_solution(16249120453141931958)
XLA Ops:
  1.3 0.0 copy-start
  1.3 1.6 %copy-done = bf16[256,4096]{1,0:T(8,128)(2,1)S(1)} copy-done((bf16[256,4096]{1,0:T(8,128)(2,1)S(1)}, bf16[256,4096]{1,0:T(8,128)(2,1)}, u32[]{:S(2)}) %copy-start) | copy-done | bytes 2097176
  2.9 0.0 copy-start.1
  2.9 0.8 %copy-done.1 = bf16[128,256]{1,0:T(8,128)(2,1)S(1)} copy-done((bf16[128,256]{1,0:T(8,128)(2,1)S(1)}, bf16[128,256]{1,0:T(8,128)(2,1)}, u32[]{:S(2)}) %copy-start.1) | copy-done | bytes 65560
  3.7 0.0 copy-start.2
  3.7 0.8 %copy-done.2 = bf16[128,256]{1,0:T(8,128)(2,1)S(1)} copy-done((bf16[128,256]{1,0:T(8,128)(2,1)S(1)}, bf16[128,256]{1,0:T(8,128)(2,1)}, u32[]{:S(2)}) %copy-start.2) | copy-done | bytes 65560
  4.6 0.0 copy-start.3
  4.6 0.8 %copy-done.3 = bf16[128,256]{1,0:T(8,128)(2,1)S(1)} copy-done((bf16[128,256]{1,0:T(8,128)(2,1)S(1)}, bf16[128,256]{1,0:T(8,128)(2,1)}, u32[]{:S(2)}) %copy-start.3) | copy-done | bytes 65560
  5.4 0.0 copy-start.4
  5.4 0.8 %copy-done.4 = bf16[128,256]{1,0:T(8,128)(2,1)S(1)} copy-done((bf16[128,256]{1,0:T(8,128)(2,1)S(1)}, bf16[128,256]{1,0:T(8,128)(2,1)}, u32[]{:S(2)}) %copy-start.4) | copy-done | bytes 65560
  6.2 0.0 copy-start.5
  6.2 0.8 %copy-done.5 = bf16[128,256]{1,0:T(8,128)(2,1)S(1)} copy-done((bf16[128,256]{1,0:T(8,128)(2,1)S(1)}, bf16[128,256]{1,0:T(8,128)(2,1)}, u32[]{:S(2)}) %copy-start.5) | copy-done | bytes 65560
  7.1 0.0 copy-start.6
  7.1 0.7 copy-done.6
  7.7 59.6 %shard_map.103 = (bf16[128,256]{1,0:T(8,128)(2,1)S(1)}, bf16[128,256]{1,0:T(8,128)(2,1)S(1)}, bf16[128,256]{1,0:T(8,128)(2,1)S(1)}) custom-call(s32[1]{0:T(128)S(6)} %copy.14.prefix_ref, s32[64]{0:T(128)S(1)} %copy-done.6, bf16[128,256]{1,0:T(8,128)(2,1)S(1)} %copy-done.1, bf16[128,256]{1,0:T(8,128)(2,1)S(1)} %copy-done.2, bf16[128,256]{1,0:T(8,128)(2,1)S(1)} %copy-done.3, ...), custom_call_target="tpu_custom_call" | custom-call | tf_op jit(solution)/shard_map/pallas_call | solution.py:396
  67.3 0.6 copy.15
  68.0 0.6 copy.16
  68.6 0.6 copy.17
Async XLA Ops:
  1.3 1.6 %copy-start = (bf16[256,4096]{1,0:T(8,128)(2,1)S(1)}, bf16[256,4096]{1,0:T(8,128)(2,1)}, u32[]{:S(2)}) copy-start(bf16[256,4096]{1,0:T(8,128)(2,1)} %w_hbm.1) | copy-start | bytes 6291460
  2.9 0.8 %copy-start.1 = (bf16[128,256]{1,0:T(8,128)(2,1)S(1)}, bf16[128,256]{1,0:T(8,128)(2,1)}, u32[]{:S(2)}) copy-start(bf16[128,256]{1,0:T(8,128)(2,1)} %q_hbm.1) | copy-start | bytes 196612
  3.7 0.8 %copy-start.2 = (bf16[128,256]{1,0:T(8,128)(2,1)S(1)}, bf16[128,256]{1,0:T(8,128)(2,1)}, u32[]{:S(2)}) copy-start(bf16[128,256]{1,0:T(8,128)(2,1)} %k_hbm.1) | copy-start | bytes 196612
  4.6 0.8 %copy-start.3 = (bf16[128,256]{1,0:T(8,128)(2,1)S(1)}, bf16[128,256]{1,0:T(8,128)(2,1)}, u32[]{:S(2)}) copy-start(bf16[128,256]{1,0:T(8,128)(2,1)} %v_hbm.1) | copy-start | bytes 196612
  5.4 0.8 %copy-start.4 = (bf16[128,256]{1,0:T(8,128)(2,1)S(1)}, bf16[128,256]{1,0:T(8,128)(2,1)}, u32[]{:S(2)}) copy-start(bf16[128,256]{1,0:T(8,128)(2,1)} %o_hbm.1) | copy-start | bytes 196612
  6.2 0.8 %copy-start.5 = (bf16[128,256]{1,0:T(8,128)(2,1)S(1)}, bf16[128,256]{1,0:T(8,128)(2,1)}, u32[]{:S(2)}) copy-start(bf16[128,256]{1,0:T(8,128)(2,1)} %d_hbm.1) | copy-start | bytes 196612
  7.1 0.7 copy-start.6

commit v2 on v1

v2 whole, which is shorter than its diff:
```python
import functools

import jax
import jax.numpy as jnp
from jax import lax
from jax.experimental import pallas as pl
from jax.experimental.pallas import tpu as pltpu
from jax.sharding import PartitionSpec as P

MESH = pl.DeviceIdType.MESH
F32 = jnp.float32
BF16 = jnp.bfloat16

HD = 256
ROWS = 128
HALF = ROWS // 2
NZ = 8
NJ = 4
NH = 4
FLOOR = -1e30
SCALE = HD ** -0.5
MESSAGES = 87


def nt(a, b):
    return lax.dot_general(a, b, (((1,), (1,)), ((), ())), preferred_element_type=F32)


def nn(a, b):
    return lax.dot_general(a, b, (((1,), (0,)), ((), ())), preferred_element_type=F32)


def tn(a, b):
    return lax.dot_general(a, b, (((0,), (0,)), ((), ())), preferred_element_type=F32)


def rows(slot, count=ROWS, first=0):
    return pl.ds(slot * ROWS + first, count)


def kernel(
    prefix_ref,
    order_hbm,
    q_hbm,
    k_hbm,
    v_hbm,
    o_hbm,
    d_hbm,
    w_hbm,
    dq_out,
    dk_out,
    dv_out,
    order_ref,
    qb,
    kb,
    vb,
    ob,
    dl,
    wb,
    gb,
    tops,
    sums,
    st,
    delta,
    score,
    prob,
    ds,
    dv_acc,
    dk_acc,
    dq_acc,
    dv_send,
    dk_send,
    dv_recv,
    dk_recv,
    dq_send,
    dq_recv,
    local_sem,
    send_sem,
    recv_sem,
):
    blk = lax.axis_index("blk")
    head = lax.axis_index("head")
    z, j = lax.div(blk, NJ), lax.rem(blk, NJ)
    yh, x = lax.div(head, NH), lax.rem(head, NH)

    def at_z(step):
        return (lax.rem(z + (step + NZ), NZ) * NJ + j, head)

    def at_y(step):
        return (blk, lax.rem(yh + (step + NH), NH) * NH + x)

    def at_x(step):
        return (blk, yh * NH + lax.rem(x + (step + NH), NH))

    core_peer = (z * NJ + j + 1 - 2 * lax.rem(j, 2), head)
    pair_peer = (z * NJ + j + 2 - 4 * lax.div(j, 2), head)

    barrier = pltpu.get_barrier_semaphore()
    neighbours = (at_z(1), at_z(-1), at_y(1), at_y(-1), at_x(1), at_x(-1), core_peer, pair_peer)
    for device in neighbours:
        pl.semaphore_signal(barrier, inc=1, device_id=device, device_id_type=MESH)

    loads = {}

    def load(name, src, dst):
        copy = pltpu.make_async_copy(src, dst, local_sem.at[len(loads)])
        copy.start()
        loads[name] = copy

    load("k", k_hbm, kb.at[rows(0)])
    load("q", q_hbm, qb.at[rows(0)])
    load("d", d_hbm, dl.at[rows(0)])
    load("w", w_hbm, wb)
    load("order", order_hbm, order_ref)
    load("v", v_hbm, vb.at[rows(0)])
    load("o", o_hbm, ob)
    pl.semaphore_wait(barrier, len(neighbours))

    sent = {}
    unfinished = []

    def send(name, src, dst, device):
        index = len(sent)
        copy = pltpu.make_async_remote_copy(
            src_ref=src,
            dst_ref=dst,
            send_sem=send_sem.at[index],
            recv_sem=recv_sem.at[index],
            device_id=device,
            device_id_type=MESH,
        )
        copy.start()
        sent[name] = copy
        unfinished.append(copy)

    def arrived(*names):
        for name in names:
            sent[name].wait_recv()

    def settle():
        while unfinished:
            unfinished.pop().wait_send()

    LOW, HIGH = 0, 1

    def half(slot, which):
        return rows(slot, HALF, which * HALF)

    def slot_of(dy, dx):
        return (dy % NH) * NH + dx % NH

    def y_start(which, way):
        send(("y", way, which), d_hbm.at[half(0, which)], dl.at[half(slot_of(-way, 0), which)], at_y(way))

    def y_relay(way):
        which = LOW if way == 1 else HIGH
        arrived(("y", way, which))
        send(("yy", way), dl.at[half(slot_of(-way, 0), which)], dl.at[half(slot_of(2, 0), which)], at_y(way))

    def x_start(dy, which, way):
        block = half(slot_of(dy, 0), which)
        src = dl.at[block] if dy else d_hbm.at[block]
        send(("x", way, dy, which), src, dl.at[half(slot_of(dy, -way), which)], at_x(way))

    def x_both(dy, which):
        x_start(dy, which, 1 if which == LOW else -1)
        x_start(dy, which, -1 if which == LOW else 1)

    def x_relay(dy, way):
        which = LOW if way == 1 else HIGH
        arrived(("x", way, dy, which))
        send(("xx", way, dy), dl.at[half(slot_of(dy, -way), which)], dl.at[half(slot_of(dy, 2), which)], at_x(way))

    def z_step(kind, hbm, buf, step):
        for way in (1, -1):
            near = (-way * step) % NZ
            if step:
                arrived((kind, way, step - 1))
            if step < 3:
                src = buf.at[rows(near)] if step else hbm
                send((kind, way, step), src, buf.at[rows((near - way) % NZ)], at_z(way))
            else:
                which = LOW if way == 1 else HIGH
                send((kind, way, step), buf.at[half(near, which)], buf.at[half(4, which)], at_z(way))

    y_start(LOW, 1)
    y_start(HIGH, -1)
    z_step("k", k_hbm, kb, 0)
    x_both(0, LOW)
    x_both(0, HIGH)
    y_start(HIGH, 1)
    y_start(LOW, -1)
    send("q core", q_hbm, qb.at[rows(1)], core_peer)
    send("q pair", q_hbm, qb.at[rows(2)], pair_peer)
    z_step("v", v_hbm, vb, 0)

    loads["order"].wait()
    lane = lax.broadcasted_iota(jnp.int32, (1, ROWS), 1)
    sub = lax.broadcasted_iota(jnp.int32, (ROWS, 1), 0)

    def block_positions(index, iota):
        first, second = order_ref[2 * index], order_ref[2 * index + 1]
        return jnp.where(iota < HALF, first * HALF + iota, second * HALF + iota - HALF)

    group = (
        blk,
        z * NJ + j + 1 - 2 * lax.rem(j, 2),
        z * NJ + j + 2 - 4 * lax.div(j, 2),
        z * NJ + 3 - j,
    )
    reach = jnp.concatenate([block_positions(member, lane) for member in group], axis=1)
    reach = jnp.maximum(reach, prefix_ref[0] - 1)

    def score_block(dz):
        scores = nt(kb[rows(dz)], qb[...]) * SCALE
        key_pos = block_positions(lax.rem(z + dz, NZ) * NJ + j, sub)
        scores = jnp.where(key_pos <= reach, scores, FLOOR)
        top = jnp.max(scores, axis=0, keepdims=True)
        weights = jnp.exp(scores - top)
        score[rows(dz)] = weights
        tops[dz:dz + 1] = top
        sums[dz:dz + 1] = jnp.sum(weights, axis=0, keepdims=True)

    def project(*slots):
        total = None
        for dy, dx in slots:
            source = lax.rem(yh + dy % NH, NH) * NH + lax.rem(x + dx % NH, NH)
            columns = pl.ds(pl.multiple_of(source * HD, HD), HD)
            term = nt(dl[rows(slot_of(dy, dx))], wb[:, columns])
            total = term if total is None else total + term
        return total

    x_relay(0, 1)
    x_relay(0, -1)
    z_step("k", k_hbm, kb, 1)
    loads["w"].wait()
    loads["d"].wait()
    grad = project((0, 0))
    y_relay(1)
    x_both(3, LOW)
    y_relay(-1)
    x_both(1, HIGH)
    z_step("v", v_hbm, vb, 1)
    arrived(("x", 1, 0, HIGH), ("x", -1, 0, LOW))
    grad = grad + project((0, 1), (0, 3))
    arrived(("y", 1, HIGH))
    x_both(3, HIGH)
    arrived(("y", -1, LOW))
    x_both(1, LOW)
    arrived("q pair")
    send("q on", qb.at[rows(2)], qb.at[rows(3)], core_peer)
    arrived(("xx", 1, 0), ("xx", -1, 0))
    grad = grad + project((0, 2), (1, 0), (3, 0))
    x_relay(3, 1)
    x_relay(1, -1)
    z_step("k", k_hbm, kb, 2)
    loads["q"].wait()
    loads["k"].wait()
    arrived("q core", "q on")
    score_block(0)
    score_block(1)
    arrived(("yy", -1))
    x_both(2, HIGH)
    arrived(("yy", 1))
    x_both(2, LOW)
    x_relay(3, -1)
    x_relay(1, 1)
    z_step("v", v_hbm, vb, 2)
    score_block(7)
    score_block(2)
    score_block(6)
    z_step("k", k_hbm, kb, 3)
    arrived(("x", 1, 1, HIGH), ("x", -1, 1, LOW), ("x", 1, 3, HIGH), ("x", -1, 3, LOW))
    grad = grad + project((1, 1), (1, 3), (3, 1), (3, 3))
    x_relay(2, -1)
    x_relay(2, 1)
    score_block(3)
    score_block(5)
    arrived(("xx", 1, 3), ("xx", -1, 3), ("xx", 1, 1), ("xx", -1, 1))
    grad = grad + project((1, 2), (3, 2), (2, 0))
    z_step("v", v_hbm, vb, 3)
    arrived(("k", 1, 3), ("k", -1, 3))
    score_block(4)

    def swapped(row, distance):
        parts = [row[:, (member ^ distance) * ROWS:((member ^ distance) + 1) * ROWS] for member in range(NJ)]
        return jnp.concatenate(parts, axis=1)

    def offer(step, name, device, top, total):
        st[2 * step] = jnp.concatenate([jnp.broadcast_to(top, (4, NJ * ROWS)), jnp.broadcast_to(total, (4, NJ * ROWS))], axis=0)
        send(name, st.at[2 * step], st.at[2 * step + 1], device)

    def merge(step, name, distance, top, total):
        arrived(name)
        other_top = swapped(st[2 * step + 1, 0:1], distance)
        other_total = swapped(st[2 * step + 1, 4:5], distance)
        new_top = jnp.maximum(top, other_top)
        return new_top, total * jnp.exp(top - new_top) + other_total * jnp.exp(other_top - new_top)

    top = jnp.max(tops[...], axis=0, keepdims=True)
    total = jnp.sum(sums[...] * jnp.exp(tops[...] - top), axis=0, keepdims=True)
    offer(0, "s core", core_peer, top, total)
    arrived(("x", 1, 2, HIGH), ("x", -1, 2, LOW))
    grad = grad + project((2, 1), (2, 3))
    top, total = merge(0, "s core", 1, top, total)
    offer(1, "s pair", pair_peer, top, total)
    arrived(("xx", 1, 2), ("xx", -1, 2))
    grad_low = (grad + project((2, 2))).astype(BF16)
    gb[rows(0)] = grad_low
    send("g pair", gb.at[rows(0)], gb.at[rows(2)], pair_peer)
    send("g core", gb.at[rows(0)], gb.at[rows(1)], core_peer)
    loads["o"].wait()
    products = grad_low.astype(F32) * ob[...].astype(F32)
    ones = jnp.ones((8, HD), F32)
    delta[0] = lax.dot_general(
        ones, products, (((1,), (1,)), ((), ())), precision=lax.Precision.HIGHEST, preferred_element_type=F32
    )
    send("t pair", delta.at[0], delta.at[2], pair_peer)
    send("t core", delta.at[0], delta.at[1], core_peer)

    top, total = merge(1, "s pair", 2, top, total)
    tops[...] = jnp.exp(tops[...] - (top + jnp.log(total)))

    def make_prob(dz):
        probs = score[rows(dz)] * tops[dz:dz + 1]
        score[rows(dz)] = probs
        prob[rows(dz)] = probs.astype(BF16)

    for dz in range(NZ):
        make_prob(dz)
    arrived(("v", 1, 3), ("v", -1, 3))
    loads["v"].wait()

    def pair_terms(pair, here, delta_row):
        columns = pl.ds(2 * ROWS * pair, 2 * ROWS)
        grad_pair = gb[columns]
        grad_probs = nt(vb[here], grad_pair)
        grad_scores = (score[here, columns] * (grad_probs - delta_row) * SCALE).astype(BF16)
        ds[here, columns] = grad_scores
        return nn(prob[here, columns], grad_pair), nn(grad_scores, qb[columns])

    arrived("g core", "t core")
    delta_row = jnp.concatenate([delta[0, 0:1], delta[1, 0:1]], axis=1)

    def first_pair(dz):
        here = rows(dz)
        dv, dk = pair_terms(0, here, delta_row)
        dv_acc[here] = dv
        dk_acc[here] = dk

    for dz in (4, 5, 3, 6):
        first_pair(dz)
    arrived("g pair")
    send("g on", gb.at[rows(2)], gb.at[rows(3)], core_peer)
    arrived("t pair")
    send("t on", delta.at[2], delta.at[3], core_peer)
    for dz in (2, 7, 1, 0):
        first_pair(dz)
    arrived("g on", "t on")
    delta_far = jnp.concatenate([delta[2, 0:1], delta[3, 0:1]], axis=1)

    def second_pair(dz):
        here = rows(dz)
        dv, dk = pair_terms(1, here, delta_far)
        dv_acc[here] = dv_acc[here] + dv
        dk_acc[here] = dk_acc[here] + dk

    def pass_on(kind, acc, out, recv, dz, way, first):
        for which in (LOW, HIGH):
            here = half(dz, which)
            value = acc[here]
            if not first:
                arrived((kind, way, dz, which))
                value = value + recv[here].astype(F32)
            out[here] = value.astype(BF16)
            target = (dz - way) % NZ
            landing = 4 if target == 0 and way == (1 if kind == "dv" else -1) else target
            send((kind, way, target, which), out.at[here], recv.at[half(landing, which)], at_z(way))

    dv_pass = functools.partial(pass_on, "dv", dv_acc, dv_send, dv_recv)
    dk_pass = functools.partial(pass_on, "dk", dk_acc, dk_send, dk_recv)

    def query_term(slot):
        return tn(ds[:, slot * ROWS:(slot + 1) * ROWS], kb[...])

    def query_pair(slot):
        dq_send[rows(slot - 2)] = query_term(slot).astype(BF16)

    second_pair(4)
    dv_pass(4, -1, True)
    dk_pass(4, 1, True)
    second_pair(5)
    dk_pass(5, -1, True)
    second_pair(3)
    dv_pass(3, 1, True)
    second_pair(2)
    second_pair(6)
    dv_pass(5, -1, False)
    dk_pass(3, 1, False)
    second_pair(7)
    second_pair(1)
    dk_pass(6, -1, False)
    dv_pass(2, 1, False)
    second_pair(0)
    query_pair(2)
    dv_pass(6, -1, False)
    dk_pass(2, 1, False)
    query_pair(3)
    send("dq pair", dq_send.at[pl.ds(0, 2 * ROWS)], dq_recv.at[pl.ds(0, 2 * ROWS)], pair_peer)
    dk_pass(7, -1, False)
    dv_pass(1, 1, False)
    dq_acc[rows(1)] = query_term(1)
    dv_pass(7, -1, False)
    dk_pass(1, 1, False)
    dq_acc[rows(0)] = query_term(0)
    arrived("dq pair")
    dq_send[rows(2)] = (dq_acc[rows(1)] + dq_recv[rows(1)].astype(F32)).astype(BF16)
    send("dq core", dq_send.at[rows(2)], dq_recv.at[rows(2)], core_peer)
    dq = dq_acc[rows(0)] + dq_recv[rows(0)].astype(F32)
    settle()
    arrived("dq core")
    dq_out[...] = (dq + dq_recv[rows(2)].astype(F32)).astype(BF16)

    def own(kind, acc, recv, out, which):
        arrived((kind, 1, 0, which), (kind, -1, 0, which))
        ahead, behind = recv[half(0, which)].astype(F32), recv[half(4, which)].astype(F32)
        out[half(0, which)] = (acc[half(0, which)] + ahead + behind).astype(BF16)

    for which in (LOW, HIGH):
        own("dv", dv_acc, dv_recv, dv_out, which)
        own("dk", dk_acc, dk_recv, dk_out, which)


def shards(queries, keys, values, saved_out, d_layer, out_weight, prefix, block_order):
    block = jax.ShapeDtypeStruct((ROWS, HD), BF16)
    anywhere = pl.BlockSpec(memory_space=pl.ANY)
    vmem = pl.BlockSpec(memory_space=pltpu.VMEM)
    operands = (block_order, queries, keys, values, saved_out, d_layer, out_weight)
    return pl.pallas_call(
        kernel,
        out_shape=(block, block, block),
        in_specs=[pl.BlockSpec(memory_space=pltpu.SMEM)] + [anywhere] * 7,
        out_specs=(vmem, vmem, vmem),
        scratch_shapes=[
            pltpu.SMEM((2 * NZ * NJ,), jnp.int32),
            pltpu.VMEM((NJ * ROWS, HD), BF16),
            pltpu.VMEM((NZ * ROWS, HD), BF16),
            pltpu.VMEM((NZ * ROWS, HD), BF16),
            pltpu.VMEM((ROWS, HD), BF16),
            pltpu.VMEM((NH * NH * ROWS, HD), BF16),
            pltpu.VMEM((HD, NH * NH * HD), BF16),
            pltpu.VMEM((NJ * ROWS, HD), BF16),
            pltpu.VMEM((NZ, NJ * ROWS), F32),
            pltpu.VMEM((NZ, NJ * ROWS), F32),
            pltpu.VMEM((4, 8, NJ * ROWS), F32),
            pltpu.VMEM((NJ, 8, ROWS), F32),
            pltpu.VMEM((NZ * ROWS, NJ * ROWS), F32),
            pltpu.VMEM((NZ * ROWS, NJ * ROWS), BF16),
            pltpu.VMEM((NZ * ROWS, NJ * ROWS), BF16),
            pltpu.VMEM((NZ * ROWS, HD), F32),
            pltpu.VMEM((NZ * ROWS, HD), F32),
            pltpu.VMEM((2 * ROWS, HD), F32),
            pltpu.VMEM((NZ * ROWS, HD), BF16),
            pltpu.VMEM((NZ * ROWS, HD), BF16),
            pltpu.VMEM((NZ * ROWS, HD), BF16),
            pltpu.VMEM((NZ * ROWS, HD), BF16),
            pltpu.VMEM((3 * ROWS, HD), BF16),
            pltpu.VMEM((3 * ROWS, HD), BF16),
            pltpu.SemaphoreType.DMA((7,)),
            pltpu.SemaphoreType.DMA((MESSAGES,)),
            pltpu.SemaphoreType.DMA((MESSAGES,)),
        ],
        compiler_params=pltpu.CompilerParams(
            collective_id=0, has_side_effects=True, vmem_limit_bytes=48 * 1024 * 1024
        ),
    )(prefix, *[pltpu.with_memory_space_constraint(operand, pltpu.HBM) for operand in operands])


def solution(mesh):
    tokens = P("blk", "head")
    return jax.shard_map(
        shards,
        mesh=mesh,
        in_specs=(tokens, tokens, tokens, tokens, tokens, P("head", None), P(), P()),
        out_specs=(tokens, tokens, tokens),
        check_vma=False,
    )
```

time: 69.6 us -> 55.2 us (0.79)
  Pallas kernels: 59.6 us -> 51.9 us
  local copies, waits for them, and re-layouts: 8.32 us -> 1.89 us
    pallas_call x1, Pallas kernels: 59.6 us -> 51.9 us  [shards(): pl.pallas_call(kernel, out_shape=(block, block, block), in_specs=[pl.Bloc...]
    unnamed x17 -> x3, local copies, waits for them, and re-layouts: 8.32 us -> 1.89 us
where the time goes in v2:
time: 55.2 us; the launch traced here: 55.1 us
  Pallas kernels  51.9 us (94%)
  local copies, waits for them, and re-layouts  1.89 us (3%)
  between operations  1.29 us (2%)
    pallas_call x1, Pallas kernels, shards(): pl.pallas_call(kernel, out_shape=(block, block, block), in_specs=[pl.Bloc...  51.9 us
    unnamed x3, local copies, waits for them, and re-layouts  1.89 us

profile of v2, /device:TPU:1, one launch (start us, length us, event | category | flops | bytes accessed | tf_op | source)
XLA Modules:
  0.0 55.1 jit_solution(14835125644603240478)
XLA Ops:
  1.3 51.9 %shard_map.103 = (bf16[128,256]{1,0:T(8,128)(2,1)S(1)}, bf16[128,256]{1,0:T(8,128)(2,1)S(1)}, bf16[128,256]{1,0:T(8,128)(2,1)S(1)}) custom-call(s32[1]{0:T(128)S(6)} %copy.14.prefix_ref, s32[64]{0:T(128)} %order_hbm.1, bf16[128,256]{1,0:T(8,128)(2,1)} %q_hbm.1, bf16[128,256]{1,0:T(8,128)(2,1)} %k_hbm.1, bf16[128,256]{1,0:T(8,128)(2,1)} %v_hbm.1, ...), custom_call_target="tpu_custom_call" | custom-call | tf_op jit(solution)/shard_map/pallas_call | solution.py:439
  53.2 0.6 %copy.15 = bf16[128,256]{1,0:T(8,128)(2,1)} copy(bf16[128,256]{1,0:T(8,128)(2,1)S(1)} %get-tuple-element.6) | data formatting | bytes 131072
  53.8 0.6 %copy.16 = bf16[128,256]{1,0:T(8,128)(2,1)} copy(bf16[128,256]{1,0:T(8,128)(2,1)S(1)} %get-tuple-element.7) | data formatting | bytes 131072
  54.4 0.6 %copy.17 = bf16[128,256]{1,0:T(8,128)(2,1)} copy(bf16[128,256]{1,0:T(8,128)(2,1)S(1)} %get-tuple-element.8) | data formatting | bytes 131072

commit v3 on v2

v3 whole, which is shorter than its diff:
```python
import functools

import jax
import jax.numpy as jnp
from jax import lax
from jax.experimental import pallas as pl
from jax.experimental.pallas import tpu as pltpu
from jax.sharding import PartitionSpec as P

MESH = pl.DeviceIdType.MESH
F32 = jnp.float32
BF16 = jnp.bfloat16

HD = 256
ROWS = 128
HALF = ROWS // 2
NZ = 8
NJ = 4
NH = 4
FLOOR = -1e30
SCALE = HD ** -0.5
MESSAGES = 100


def nt(a, b):
    return lax.dot_general(a, b, (((1,), (1,)), ((), ())), preferred_element_type=F32)


def nn(a, b):
    return lax.dot_general(a, b, (((1,), (0,)), ((), ())), preferred_element_type=F32)


def tn(a, b):
    return lax.dot_general(a, b, (((0,), (0,)), ((), ())), preferred_element_type=F32)


def rows(slot, count=ROWS, first=0):
    return pl.ds(slot * ROWS + first, count)


def kernel(
    prefix_ref,
    order_hbm,
    q_hbm,
    k_hbm,
    v_hbm,
    o_hbm,
    d_hbm,
    w_hbm,
    out,
    order_ref,
    qb,
    kb,
    vb,
    ob,
    dl,
    wb,
    gb,
    tops,
    sums,
    st,
    delta,
    score,
    prob,
    ds,
    dv_acc,
    dk_acc,
    dq_acc,
    dv_send,
    dk_send,
    dv_recv,
    dk_recv,
    dq_send,
    dq_recv,
    local_sem,
    send_sem,
    recv_sem,
):
    dq_out, dk_out, dv_out = out.at[0], out.at[1], out.at[2]
    blk = lax.axis_index("blk")
    head = lax.axis_index("head")
    z, j = lax.div(blk, NJ), lax.rem(blk, NJ)
    yh, x = lax.div(head, NH), lax.rem(head, NH)

    def at_z(step):
        return (lax.rem(z + (step + NZ), NZ) * NJ + j, head)

    def at_y(step):
        return (blk, lax.rem(yh + (step + NH), NH) * NH + x)

    def at_x(step):
        return (blk, yh * NH + lax.rem(x + (step + NH), NH))

    core_peer = (z * NJ + j + 1 - 2 * lax.rem(j, 2), head)
    pair_peer = (z * NJ + j + 2 - 4 * lax.div(j, 2), head)
    far_peer = (z * NJ + NJ - 1 - j, head)

    barrier = pltpu.get_barrier_semaphore()
    neighbours = (at_z(1), at_z(-1), at_y(1), at_y(-1), at_x(1), at_x(-1), core_peer, pair_peer, far_peer)
    for device in neighbours:
        pl.semaphore_signal(barrier, inc=1, device_id=device, device_id_type=MESH)

    loads = {}

    def load(name, src, dst):
        copy = pltpu.make_async_copy(src, dst, local_sem.at[len(loads)])
        copy.start()
        loads[name] = copy

    load("d", d_hbm, dl.at[rows(0)])
    load("k", k_hbm, kb.at[rows(0)])
    load("q", q_hbm, qb.at[rows(0)])
    load("v", v_hbm, vb.at[rows(0)])
    load("order", order_hbm, order_ref)
    load("w", w_hbm, wb)
    load("o", o_hbm, ob)
    for name in ("d", "k", "q", "v"):
        loads[name].wait()
    pl.semaphore_wait(barrier, len(neighbours))

    sent = {}
    unfinished = []

    def send(name, src, dst, device):
        index = len(sent)
        copy = pltpu.make_async_remote_copy(
            src_ref=src,
            dst_ref=dst,
            send_sem=send_sem.at[index],
            recv_sem=recv_sem.at[index],
            device_id=device,
            device_id_type=MESH,
        )
        copy.start()
        sent[name] = copy
        unfinished.append(copy)

    taken = set()

    def arrived(*names):
        for name in names:
            if name not in taken:
                taken.add(name)
                sent[name].wait_recv()

    def settle():
        while unfinished:
            unfinished.pop().wait_send()

    LOW, HIGH = 0, 1

    def half(slot, which):
        return rows(slot, HALF, which * HALF)

    def slot_of(dy, dx):
        return (dy % NH) * NH + dx % NH

    def y_start(which, way):
        send(("y", way, which), dl.at[half(0, which)], dl.at[half(slot_of(-way, 0), which)], at_y(way))

    def x_start(dy, which, way):
        block = half(slot_of(dy, 0), which)
        send(("x", way, dy, which), dl.at[block], dl.at[half(slot_of(dy, -way), which)], at_x(way))

    def x_both(dy, which):
        x_start(dy, which, 1 if which == LOW else -1)
        x_start(dy, which, -1 if which == LOW else 1)

    def y_relay(way):
        which = LOW if way == 1 else HIGH
        arrived(("y", way, which))
        send(("yy", way), dl.at[half(slot_of(-way, 0), which)], dl.at[half(slot_of(2, 0), which)], at_y(way))
        x_both((-way) % NH, which)

    def y_rest(way):
        which = HIGH if way == 1 else LOW
        arrived(("y", way, which))
        x_both((-way) % NH, which)

    def y_far(way):
        arrived(("yy", way))
        x_both(2, LOW if way == 1 else HIGH)

    def x_relay(dy, way):
        which = LOW if way == 1 else HIGH
        arrived(("x", way, dy, which))
        send(("xx", way, dy), dl.at[half(slot_of(dy, -way), which)], dl.at[half(slot_of(dy, 2), which)], at_x(way))

    stores = {"k": kb, "v": vb}

    def z_send(kind, step, way, which, src):
        near = (-way * step) % NZ
        send((kind, way, step, which), src, stores[kind].at[half((near - way) % NZ, which)], at_z(way))

    def z_start(kind, which):
        own = stores[kind]
        z_send(kind, 0, 1, which, own.at[half(0, which)])
        z_send(kind, 0, -1, 1 - which, own.at[half(0, 1 - which)])

    def z_relay(kind, step, way, which):
        arrived((kind, way, step - 1, which))
        z_send(kind, step, way, which, stores[kind].at[half((-way * step) % NZ, which)])

    y_start(LOW, 1)
    y_start(HIGH, -1)
    z_start("k", LOW)
    x_both(0, LOW)
    x_both(0, HIGH)
    z_start("k", HIGH)
    y_start(HIGH, 1)
    y_start(LOW, -1)
    send("q core", qb.at[rows(0)], qb.at[rows(1)], core_peer)
    z_start("v", LOW)
    z_start("v", HIGH)

    loads["order"].wait()
    lane = lax.broadcasted_iota(jnp.int32, (1, ROWS), 1)
    sub = lax.broadcasted_iota(jnp.int32, (ROWS, 1), 0)

    def block_positions(index, iota):
        first, second = order_ref[2 * index], order_ref[2 * index + 1]
        return jnp.where(iota < HALF, first * HALF + iota, second * HALF + iota - HALF)

    group = (
        blk,
        z * NJ + j + 1 - 2 * lax.rem(j, 2),
        z * NJ + j + 2 - 4 * lax.div(j, 2),
        z * NJ + 3 - j,
    )
    reach = jnp.concatenate([block_positions(member, lane) for member in group], axis=1)
    reach = jnp.maximum(reach, prefix_ref[0] - 1)

    def key_arrival(kind, dz):
        if dz == 0:
            return ()
        if dz == NZ // 2:
            return (kind, 1, 3, LOW), (kind, -1, 3, HIGH)
        way, step = (1, NZ - 1 - dz) if dz > NZ // 2 else (-1, dz - 1)
        return (kind, way, step, LOW), (kind, way, step, HIGH)

    def score_block(dz):
        arrived(*key_arrival("k", dz))
        scores = nt(kb[rows(dz)], qb[...]) * SCALE
        key_pos = block_positions(lax.rem(z + dz, NZ) * NJ + j, sub)
        scores = jnp.where(key_pos <= reach, scores, FLOOR)
        top = jnp.max(scores, axis=0, keepdims=True)
        weights = jnp.exp(scores - top)
        score[rows(dz)] = weights
        tops[dz:dz + 1] = top
        sums[dz:dz + 1] = jnp.sum(weights, axis=0, keepdims=True)

    def arrival(dy, dx):
        if dx == 2:
            return ("xx", 1, dy), ("xx", -1, dy)
        if dx:
            way = 1 if dx == 3 else -1
            return ("x", way, dy, LOW), ("x", way, dy, HIGH)
        return ()

    def project(dy, dx):
        arrived(*arrival(dy, dx))
        source = lax.rem(yh + dy, NH) * NH + lax.rem(x + dx, NH)
        columns = pl.ds(pl.multiple_of(source * HD, HD), HD)
        return nt(dl[rows(slot_of(dy, dx))], wb[:, columns])

    def offer():
        top = jnp.max(tops[...], axis=0, keepdims=True)
        total = jnp.sum(sums[...] * jnp.exp(tops[...] - top), axis=0, keepdims=True)
        wide = (4, NJ * ROWS)
        st[0] = jnp.concatenate([jnp.broadcast_to(top, wide), jnp.broadcast_to(total, wide)], axis=0)
        for distance, device in ((2, pair_peer), (3, far_peer), (1, core_peer)):
            send(("s", distance), st.at[0], st.at[distance], device)

    def statistics(distance, row):
        found = st[distance, row:row + 1]
        parts = [found[:, (member ^ distance) * ROWS:((member ^ distance) + 1) * ROWS] for member in range(NJ)]
        return jnp.concatenate(parts, axis=1)

    def merge():
        arrived(("s", 1), ("s", 2), ("s", 3))
        part_tops = [statistics(distance, 0) for distance in range(NJ)]
        top = functools.reduce(jnp.maximum, part_tops)
        total = sum(statistics(distance, 4) * jnp.exp(part_tops[distance] - top) for distance in range(NJ))
        tops[...] = jnp.exp(tops[...] - (top + jnp.log(total)))

    loads["w"].wait()
    grad = project(0, 0)
    z_relay("k", 1, 1, LOW)
    z_relay("k", 1, -1, HIGH)
    x_relay(0, 1)
    z_relay("k", 1, 1, HIGH)
    z_relay("k", 1, -1, LOW)
    x_relay(0, -1)
    grad = grad + project(0, 3)
    grad = grad + project(0, 1)
    y_relay(1)
    y_relay(-1)
    send("q pair", qb.at[rows(0)], qb.at[rows(2)], pair_peer)
    z_relay("v", 1, 1, LOW)
    z_relay("v", 1, -1, HIGH)
    z_relay("v", 1, 1, HIGH)
    z_relay("v", 1, -1, LOW)
    y_rest(1)
    y_rest(-1)
    z_relay("k", 2, 1, LOW)
    z_relay("k", 2, -1, HIGH)
    grad = grad + project(3, 0)
    grad = grad + project(1, 0)
    grad = grad + project(0, 2)
    z_relay("k", 2, 1, HIGH)
    z_relay("k", 2, -1, LOW)
    x_relay(3, 1)
    z_relay("v", 2, 1, LOW)
    z_relay("v", 2, -1, HIGH)
    arrived("q pair")
    send("q on", qb.at[rows(2)], qb.at[rows(3)], core_peer)
    arrived("q core", "q on")
    score_block(0)
    x_relay(1, -1)
    score_block(1)
    z_relay("v", 2, 1, HIGH)
    z_relay("v", 2, -1, LOW)
    y_far(-1)
    score_block(2)
    x_relay(3, -1)
    y_far(1)
    z_relay("k", 3, 1, LOW)
    z_relay("k", 3, -1, HIGH)
    score_block(6)
    x_relay(1, 1)
    score_block(7)
    grad = grad + project(3, 3)
    grad = grad + project(3, 1)
    grad = grad + project(2, 0)
    z_relay("v", 3, 1, LOW)
    z_relay("v", 3, -1, HIGH)
    grad = grad + project(1, 3)
    grad = grad + project(1, 1)
    score_block(5)
    score_block(3)
    x_relay(2, -1)
    x_relay(2, 1)
    grad = grad + project(2, 3)
    score_block(4)
    offer()
    grad = grad + project(3, 2)
    grad = grad + project(1, 2)
    grad = grad + project(2, 1)
    grad = grad + project(2, 2)
    grad_low = grad.astype(BF16)
    gb[rows(0)] = grad_low
    send("g pair", gb.at[rows(0)], gb.at[rows(2)], pair_peer)
    send("g core", gb.at[rows(0)], gb.at[rows(1)], core_peer)
    loads["o"].wait()
    products = grad_low.astype(F32) * ob[...].astype(F32)
    ones = jnp.ones((8, HD), F32)
    delta[0] = lax.dot_general(
        ones, products, (((1,), (1,)), ((), ())), precision=lax.Precision.HIGHEST, preferred_element_type=F32
    )
    for distance, device in ((2, pair_peer), (3, far_peer), (1, core_peer)):
        send(("t", distance), delta.at[0], delta.at[distance], device)
    merge()

    def make_prob(dz):
        probs = score[rows(dz)] * tops[dz:dz + 1]
        score[rows(dz)] = probs
        prob[rows(dz)] = probs.astype(BF16)

    for dz in range(NZ):
        make_prob(dz)
    for dz in range(NZ):
        arrived(*key_arrival("v", dz))

    def pair_terms(pair, here, delta_row):
        columns = pl.ds(2 * ROWS * pair, 2 * ROWS)
        grad_pair = gb[columns]
        grad_probs = nt(vb[here], grad_pair)
        grad_scores = (score[here, columns] * (grad_probs - delta_row) * SCALE).astype(BF16)
        ds[here, columns] = grad_scores
        return nn(prob[here, columns], grad_pair), nn(grad_scores, qb[columns])

    arrived("g core", ("t", 1))
    delta_row = jnp.concatenate([delta[0, 0:1], delta[1, 0:1]], axis=1)

    def first_pair(dz):
        here = rows(dz)
        dv, dk = pair_terms(0, here, delta_row)
        dv_acc[here] = dv
        dk_acc[here] = dk

    for dz in (4, 5, 3, 6):
        first_pair(dz)
    arrived("g pair")
    send("g on", gb.at[rows(2)], gb.at[rows(3)], core_peer)
    for dz in (2, 7, 1, 0):
        first_pair(dz)
    arrived("g on", ("t", 2), ("t", 3))
    delta_far = jnp.concatenate([delta[2, 0:1], delta[3, 0:1]], axis=1)

    def second_pair(dz):
        here = rows(dz)
        dv, dk = pair_terms(1, here, delta_far)
        dv_acc[here] = dv_acc[here] + dv
        dk_acc[here] = dk_acc[here] + dk

    sums_of = {"dv": (dv_acc, dv_send, dv_recv), "dk": (dk_acc, dk_send, dk_recv)}

    def pass_on(*parts):
        for which in (LOW, HIGH):
            for kind, dz, way, first in parts:
                acc, out, recv = sums_of[kind]
                here = half(dz, which)
                value = acc[here]
                if not first:
                    arrived((kind, way, dz, which))
                    value = value + recv[here].astype(F32)
                out[here] = value.astype(BF16)
                target = (dz - way) % NZ
                landing = 4 if target == 0 and way == (1 if kind == "dv" else -1) else target
                send((kind, way, target, which), out.at[here], recv.at[half(landing, which)], at_z(way))

    def query_term(slot):
        return tn(ds[:, slot * ROWS:(slot + 1) * ROWS], kb[...])

    def query_pair(slot):
        dq_send[rows(slot - 2)] = query_term(slot).astype(BF16)

    second_pair(4)
    pass_on(("dv", 4, -1, True), ("dk", 4, 1, True))
    second_pair(5)
    second_pair(3)
    pass_on(("dk", 5, -1, True), ("dv", 3, 1, True))
    second_pair(2)
    second_pair(6)
    pass_on(("dv", 5, -1, False), ("dk", 3, 1, False))
    second_pair(7)
    second_pair(1)
    pass_on(("dk", 6, -1, False), ("dv", 2, 1, False))
    second_pair(0)
    query_pair(2)
    pass_on(("dv", 6, -1, False), ("dk", 2, 1, False))
    query_pair(3)
    send("dq pair", dq_send.at[pl.ds(0, 2 * ROWS)], dq_recv.at[pl.ds(0, 2 * ROWS)], pair_peer)
    pass_on(("dk", 7, -1, False), ("dv", 1, 1, False))
    dq_acc[rows(1)] = query_term(1)
    pass_on(("dv", 7, -1, False), ("dk", 1, 1, False))
    dq_acc[rows(0)] = query_term(0)
    arrived("dq pair")
    dq_send[rows(2)] = (dq_acc[rows(1)] + dq_recv[rows(1)].astype(F32)).astype(BF16)
    send("dq core", dq_send.at[rows(2)], dq_recv.at[rows(2)], core_peer)
    dq = dq_acc[rows(0)] + dq_recv[rows(0)].astype(F32)
    settle()
    arrived("dq core")
    dq_out[...] = (dq + dq_recv[rows(2)].astype(F32)).astype(BF16)

    def own(kind, acc, recv, out, which):
        arrived((kind, 1, 0, which), (kind, -1, 0, which))
        ahead, behind = recv[half(0, which)].astype(F32), recv[half(4, which)].astype(F32)
        out[half(0, which)] = (acc[half(0, which)] + ahead + behind).astype(BF16)

    for which in (LOW, HIGH):
        own("dv", dv_acc, dv_recv, dv_out, which)
        own("dk", dk_acc, dk_recv, dk_out, which)


def shards(queries, keys, values, saved_out, d_layer, out_weight, prefix, block_order):
    block = jax.ShapeDtypeStruct((ROWS, HD), BF16)
    anywhere = pl.BlockSpec(memory_space=pl.ANY)
    vmem = pl.BlockSpec(memory_space=pltpu.VMEM)
    operands = (block_order, queries, keys, values, saved_out, d_layer, out_weight)
    results = pl.pallas_call(
        kernel,
        out_shape=jax.ShapeDtypeStruct((3, ROWS, HD), BF16),
        in_specs=[pl.BlockSpec(memory_space=pltpu.SMEM)] + [anywhere] * 7,
        out_specs=vmem,
        scratch_shapes=[
            pltpu.SMEM((2 * NZ * NJ,), jnp.int32),
            pltpu.VMEM((NJ * ROWS, HD), BF16),
            pltpu.VMEM((NZ * ROWS, HD), BF16),
            pltpu.VMEM((NZ * ROWS, HD), BF16),
            pltpu.VMEM((ROWS, HD), BF16),
            pltpu.VMEM((NH * NH * ROWS, HD), BF16),
            pltpu.VMEM((HD, NH * NH * HD), BF16),
            pltpu.VMEM((NJ * ROWS, HD), BF16),
            pltpu.VMEM((NZ, NJ * ROWS), F32),
            pltpu.VMEM((NZ, NJ * ROWS), F32),
            pltpu.VMEM((4, 8, NJ * ROWS), F32),
            pltpu.VMEM((NJ, 8, ROWS), F32),
            pltpu.VMEM((NZ * ROWS, NJ * ROWS), F32),
            pltpu.VMEM((NZ * ROWS, NJ * ROWS), BF16),
            pltpu.VMEM((NZ * ROWS, NJ * ROWS), BF16),
            pltpu.VMEM((NZ * ROWS, HD), F32),
            pltpu.VMEM((NZ * ROWS, HD), F32),
            pltpu.VMEM((2 * ROWS, HD), F32),
            pltpu.VMEM((NZ * ROWS, HD), BF16),
            pltpu.VMEM((NZ * ROWS, HD), BF16),
            pltpu.VMEM((NZ * ROWS, HD), BF16),
            pltpu.VMEM((NZ * ROWS, HD), BF16),
            pltpu.VMEM((3 * ROWS, HD), BF16),
            pltpu.VMEM((3 * ROWS, HD), BF16),
            pltpu.SemaphoreType.DMA((7,)),
            pltpu.SemaphoreType.DMA((MESSAGES,)),
            pltpu.SemaphoreType.DMA((MESSAGES,)),
        ],
        compiler_params=pltpu.CompilerParams(
            collective_id=0, has_side_effects=True, vmem_limit_bytes=48 * 1024 * 1024
        ),
    )(prefix, *[pltpu.with_memory_space_constraint(operand, pltpu.HBM) for operand in operands])
    return results[0], results[1], results[2]


def solution(mesh):
    tokens = P("blk", "head")
    return jax.shard_map(
        shards,
        mesh=mesh,
        in_specs=(tokens, tokens, tokens, tokens, tokens, P("head", None), P(), P()),
        out_specs=(tokens, tokens, tokens),
        check_vma=False,
    )
```

time: 55.2 us -> 53.5 us (0.969)
  local copies, waits for them, and re-layouts: 1.89 us -> 0.68 us
  Pallas kernels: 51.9 us -> 51.3 us
    unnamed x3 -> x0, local copies, waits for them, and re-layouts: 1.89 us -> none
    squeeze x0 -> x1, local copies, waits for them, and re-layouts: none -> 0.68 us  [shards(): return (results[0], results[1], results[2])]
where the time goes in v3:
time: 53.5 us; the launch traced here: 53.3 us
  Pallas kernels  51.3 us (96%)
  between operations  1.29 us (2%)
  local copies, waits for them, and re-layouts  0.68 us (1%)
    pallas_call x1, Pallas kernels, shards(): pl.pallas_call(kernel, out_shape=jax.ShapeDtypeStruct((3, ROWS, HD), BF16...  51.3 us

profile of v3, /device:TPU:1, one launch (start us, length us, event | category | flops | bytes accessed | tf_op | source)
XLA Modules:
  0.0 53.3 jit_solution(3026118492706948440)
XLA Ops:
  1.3 51.3 %shard_map.103 = bf16[3,128,256]{2,1,0:T(8,128)(2,1)S(1)} custom-call(s32[1]{0:T(128)S(6)} %copy.11.prefix_ref, s32[64]{0:T(128)} %order_hbm.1, bf16[128,256]{1,0:T(8,128)(2,1)} %q_hbm.1, bf16[128,256]{1,0:T(8,128)(2,1)} %k_hbm.1, bf16[128,256]{1,0:T(8,128)(2,1)} %v_hbm.1, bf16[128,256]{1,0:T(8,128)(2,1)} %o_hbm.1, bf16[128,256]{1,0:T(8,128)(2,1)} %d_hbm.1, ...), custom_call_target="tpu_custom_call" | custom-call | tf_op jit(solution)/shard_map/pallas_call | solution.py:471
  52.6 0.7 %slice_bitcast_fusion = (bf16[128,256]{1,0:T(8,128)(2,1)}, bf16[128,256]{1,0:T(8,128)(2,1)}, bf16[128,256]{1,0:T(8,128)(2,1)}) fusion(bf16[3,128,256]{2,1,0:T(8,128)(2,1)S(1)} %shard_map.103), kind=kLoop, calls=%fused_computation | loop fusion | bytes 393216 | tf_op jit(solution)/shard_map/squeeze | solution.py:509

commit v4 on v3

--- a/solution.py
+++ b/solution.py
@@ -211,7 +211,6 @@
     y_start(LOW, -1)
     send("q core", qb.at[rows(0)], qb.at[rows(1)], core_peer)
     z_start("v", LOW)
-    z_start("v", HIGH)
 
     loads["order"].wait()
     lane = lax.broadcasted_iota(jnp.int32, (1, ROWS), 1)
@@ -291,61 +290,62 @@
     z_relay("k", 1, 1, HIGH)
     z_relay("k", 1, -1, LOW)
     x_relay(0, -1)
+    z_start("v", HIGH)
     grad = grad + project(0, 3)
     grad = grad + project(0, 1)
     y_relay(1)
     y_relay(-1)
     send("q pair", qb.at[rows(0)], qb.at[rows(2)], pair_peer)
+    z_relay("k", 2, 1, LOW)
+    z_relay("k", 2, -1, HIGH)
+    y_rest(1)
+    y_rest(-1)
+    grad = grad + project(3, 0)
+    grad = grad + project(1, 0)
+    z_relay("k", 2, 1, HIGH)
+    z_relay("k", 2, -1, LOW)
     z_relay("v", 1, 1, LOW)
     z_relay("v", 1, -1, HIGH)
+    grad = grad + project(0, 2)
+    x_relay(3, 1)
+    x_relay(1, -1)
+    z_relay("k", 3, 1, LOW)
+    z_relay("k", 3, -1, HIGH)
     z_relay("v", 1, 1, HIGH)
     z_relay("v", 1, -1, LOW)
-    y_rest(1)
-    y_rest(-1)
-    z_relay("k", 2, 1, LOW)
-    z_relay("k", 2, -1, HIGH)
-    grad = grad + project(3, 0)
-    grad = grad + project(1, 0)
-    grad = grad + project(0, 2)
-    z_relay("k", 2, 1, HIGH)
-    z_relay("k", 2, -1, LOW)
-    x_relay(3, 1)
+    y_far(1)
+    y_far(-1)
+    grad = grad + project(2, 0)
+    grad = grad + project(3, 3)
+    x_relay(3, -1)
+    grad = grad + project(3, 1)
+    arrived("q pair")
+    send("q on", qb.at[rows(2)], qb.at[rows(3)], core_peer)
+    x_relay(1, 1)
+    grad = grad + project(1, 3)
+    grad = grad + project(1, 1)
     z_relay("v", 2, 1, LOW)
     z_relay("v", 2, -1, HIGH)
-    arrived("q pair")
-    send("q on", qb.at[rows(2)], qb.at[rows(3)], core_peer)
     arrived("q core", "q on")
     score_block(0)
-    x_relay(1, -1)
     score_block(1)
+    x_relay(2, 1)
+    score_block(2)
     z_relay("v", 2, 1, HIGH)
     z_relay("v", 2, -1, LOW)
-    y_far(-1)
-    score_block(2)
-    x_relay(3, -1)
-    y_far(1)
-    z_relay("k", 3, 1, LOW)
-    z_relay("k", 3, -1, HIGH)
+    score_block(3)
+    score_block(5)
+    x_relay(2, -1)
     score_block(6)
-    x_relay(1, 1)
-    score_block(7)
-    grad = grad + project(3, 3)
-    grad = grad + project(3, 1)
-    grad = grad + project(2, 0)
     z_relay("v", 3, 1, LOW)
     z_relay("v", 3, -1, HIGH)
-    grad = grad + project(1, 3)
-    grad = grad + project(1, 1)
-    score_block(5)
-    score_block(3)
-    x_relay(2, -1)
-    x_relay(2, 1)
-    grad = grad + project(2, 3)
+    score_block(7)
     score_block(4)
     offer()
+    grad = grad + project(2, 3)
+    grad = grad + project(2, 1)
+    grad = grad + project(1, 2)
     grad = grad + project(3, 2)
-    grad = grad + project(1, 2)
-    grad = grad + project(2, 1)
     grad = grad + project(2, 2)
     grad_low = grad.astype(BF16)
     gb[rows(0)] = grad_low

time: 53.5 us -> 53 us (level)
  no operation moved by 1% of the time
where the time goes in v4:
time: 53 us; the launch traced here: 52.9 us
  Pallas kernels  50.9 us (96%)
  between operations  1.29 us (2%)
  local copies, waits for them, and re-layouts  0.68 us (1%)
    pallas_call x1, Pallas kernels, shards(): pl.pallas_call(kernel, out_shape=jax.ShapeDtypeStruct((3, ROWS, HD), BF16...  50.9 us

profile of v4, /device:TPU:1, one launch (start us, length us, event | category | flops | bytes accessed | tf_op | source)
XLA Modules:
  0.0 52.9 jit_solution(18059168581279785018)
XLA Ops:
  1.3 50.9 %shard_map.103 = bf16[3,128,256]{2,1,0:T(8,128)(2,1)S(1)} custom-call(s32[1]{0:T(128)S(6)} %copy.11.prefix_ref, s32[64]{0:T(128)} %order_hbm.1, bf16[128,256]{1,0:T(8,128)(2,1)} %q_hbm.1, bf16[128,256]{1,0:T(8,128)(2,1)} %k_hbm.1, bf16[128,256]{1,0:T(8,128)(2,1)} %v_hbm.1, bf16[128,256]{1,0:T(8,128)(2,1)} %o_hbm.1, bf16[128,256]{1,0:T(8,128)(2,1)} %d_hbm.1, ...), custom_call_target="tpu_custom_call" | custom-call | tf_op jit(solution)/shard_map/pallas_call | solution.py:471
  52.2 0.7 %slice_bitcast_fusion = (bf16[128,256]{1,0:T(8,128)(2,1)}, bf16[128,256]{1,0:T(8,128)(2,1)}, bf16[128,256]{1,0:T(8,128)(2,1)}) fusion(bf16[3,128,256]{2,1,0:T(8,128)(2,1)S(1)} %shard_map.103), kind=kLoop, calls=%fused_computation | loop fusion | bytes 393216 | tf_op jit(solution)/shard_map/squeeze | solution.py:509

commit v5 on v4

--- a/solution.py
+++ b/solution.py
@@ -204,6 +204,7 @@
     y_start(LOW, 1)
     y_start(HIGH, -1)
     z_start("k", LOW)
+    send("q pair", qb.at[rows(0)], qb.at[rows(2)], pair_peer)
     x_both(0, LOW)
     x_both(0, HIGH)
     z_start("k", HIGH)
@@ -295,7 +296,6 @@
     grad = grad + project(0, 1)
     y_relay(1)
     y_relay(-1)
-    send("q pair", qb.at[rows(0)], qb.at[rows(2)], pair_peer)
     z_relay("k", 2, 1, LOW)
     z_relay("k", 2, -1, HIGH)
     y_rest(1)
@@ -304,44 +304,44 @@
     grad = grad + project(1, 0)
     z_relay("k", 2, 1, HIGH)
     z_relay("k", 2, -1, LOW)
+    arrived("q pair")
+    send("q on", qb.at[rows(2)], qb.at[rows(3)], core_peer)
     z_relay("v", 1, 1, LOW)
     z_relay("v", 1, -1, HIGH)
     grad = grad + project(0, 2)
     x_relay(3, 1)
     x_relay(1, -1)
+    arrived("q core", "q on")
+    score_block(0)
+    score_block(1)
+    score_block(7)
     z_relay("k", 3, 1, LOW)
     z_relay("k", 3, -1, HIGH)
     z_relay("v", 1, 1, HIGH)
     z_relay("v", 1, -1, LOW)
     y_far(1)
     y_far(-1)
+    score_block(2)
+    score_block(6)
     grad = grad + project(2, 0)
     grad = grad + project(3, 3)
     x_relay(3, -1)
     grad = grad + project(3, 1)
-    arrived("q pair")
-    send("q on", qb.at[rows(2)], qb.at[rows(3)], core_peer)
     x_relay(1, 1)
+    score_block(3)
+    score_block(5)
     grad = grad + project(1, 3)
     grad = grad + project(1, 1)
     z_relay("v", 2, 1, LOW)
     z_relay("v", 2, -1, HIGH)
-    arrived("q core", "q on")
-    score_block(0)
-    score_block(1)
     x_relay(2, 1)
-    score_block(2)
+    score_block(4)
+    offer()
     z_relay("v", 2, 1, HIGH)
     z_relay("v", 2, -1, LOW)
-    score_block(3)
-    score_block(5)
     x_relay(2, -1)
-    score_block(6)
     z_relay("v", 3, 1, LOW)
     z_relay("v", 3, -1, HIGH)
-    score_block(7)
-    score_block(4)
-    offer()
     grad = grad + project(2, 3)
     grad = grad + project(2, 1)
     grad = grad + project(1, 2)

time: 53 us -> 54 us (1.019)
  Pallas kernels: 50.9 us -> 51.9 us
    pallas_call x1, Pallas kernels: 50.9 us -> 51.9 us  [shards(): pl.pallas_call(kernel, out_shape=jax.ShapeDtypeStruct((3, ROWS, HD), BF16...]
where the time goes in v5:
time: 54 us; the launch traced here: 53.9 us
  Pallas kernels  51.9 us (96%)
  between operations  1.29 us (2%)
  local copies, waits for them, and re-layouts  0.68 us (1%)
    pallas_call x1, Pallas kernels, shards(): pl.pallas_call(kernel, out_shape=jax.ShapeDtypeStruct((3, ROWS, HD), BF16...  51.9 us

profile of v5, /device:TPU:1, one launch (start us, length us, event | category | flops | bytes accessed | tf_op | source)
XLA Modules:
  0.0 53.9 jit_solution(5122225823646202735)
XLA Ops:
  1.3 51.9 %shard_map.103 = bf16[3,128,256]{2,1,0:T(8,128)(2,1)S(1)} custom-call(s32[1]{0:T(128)S(6)} %copy.11.prefix_ref, s32[64]{0:T(128)} %order_hbm.1, bf16[128,256]{1,0:T(8,128)(2,1)} %q_hbm.1, bf16[128,256]{1,0:T(8,128)(2,1)} %k_hbm.1, bf16[128,256]{1,0:T(8,128)(2,1)} %v_hbm.1, bf16[128,256]{1,0:T(8,128)(2,1)} %o_hbm.1, bf16[128,256]{1,0:T(8,128)(2,1)} %d_hbm.1, ...), custom_call_target="tpu_custom_call" | custom-call | tf_op jit(solution)/shard_map/pallas_call | solution.py:471
  53.2 0.7 %slice_bitcast_fusion = (bf16[128,256]{1,0:T(8,128)(2,1)}, bf16[128,256]{1,0:T(8,128)(2,1)}, bf16[128,256]{1,0:T(8,128)(2,1)}) fusion(bf16[3,128,256]{2,1,0:T(8,128)(2,1)S(1)} %shard_map.103), kind=kLoop, calls=%fused_computation | loop fusion | bytes 393216 | tf_op jit(solution)/shard_map/squeeze | solution.py:509
